TPU v7x, 128 devices: a whole 4x4x4 slice. The times are simulated.
128 devices in a mesh: blk: 16 (over z, x), grp: 8 (over y, core).
Axes of the slice: x: 4, y: 4, z: 4, core: 2. Of those that a mesh axis runs over, the one named last changes fastest.
Arguments:
- right_side: float32 [256, 128, 256], P('blk', 'grp'), may hold values from -6 to 6
- weights: float32 [6, 256, 128, 256], P(None, 'blk', 'grp'), may hold values from 0.5 to 2
Outputs:
- solution_field: float32 [256, 128, 256], P('blk', 'grp')
- residual: float32 [256, 128, 256], P('blk', 'grp')
All inputs are finite; a program needn't handle non-finite values.
Results may differ from a plain program's by a relative error of at most 0.0003.
Values sent between devices are 32-bit elements; how exact they have to be, the bound alone decides.
A program may use at most 128 MiB of HBM per device.

v0:
```python
import jax
import jax.numpy as jnp
from jax import lax
from jax.sharding import PartitionSpec as P

LEVELS = 5
SWEEPS = 2
COARSE_SWEEPS = 8


DIRECTIONS = ((0, 1), (0, -1), (1, 1), (1, -1), (2, 1), (2, -1))
relaxation = 0.7


def with_halo(cells, sides, width):
    for axis, dim in sides:
        count = lax.axis_size(axis)
        ends = count - 1
        head = lax.slice_in_dim(cells, 0, width, axis=dim)
        tail = lax.slice_in_dim(cells, cells.shape[dim] - width, cells.shape[dim], axis=dim)
        cells = jnp.concatenate(
            [
                lax.ppermute(tail, axis, [(i, (i + 1) % count) for i in range(ends)]),
                cells,
                lax.ppermute(head, axis, [((i + 1) % count, i) for i in range(ends)]),
            ],
            axis=dim,
        )
    return cells


def cut(array, along, begin, end):
    return lax.slice_in_dim(array, begin, end, axis=along)


def moved(array, along, sense):
    length = array.shape[along]
    zeros = jnp.zeros_like(cut(array, along, 0, 1))
    if sense == 1:
        return jnp.concatenate([zeros, cut(array, along, 0, length - 1)], axis=along)
    return jnp.concatenate([cut(array, along, 1, length), zeros], axis=along)


def restrict(array):
    shape = array.shape
    lead = shape[:-3]
    blocks = array.reshape(lead + (shape[-3] // 2, 2, shape[-2] // 2, 2, shape[-1] // 2, 2))
    return blocks.mean(axis=(-5, -3, -1))


def prolong(coarse):
    depth, height, width = coarse.shape
    wide = jnp.broadcast_to(coarse[:, None, :, None, :, None], (depth, 2, height, 2, width, 2))
    return wide.reshape(depth * 2, height * 2, width * 2)


def spread_field(field, layout):
    if layout == "both":
        return with_halo(field, (("blk", 0), ("grp", 1)), 1)
    return with_halo(field, (("blk", 0),), 1)


def neighbour(padded, along, sense, layout, field):
    size_first = field.shape[0]
    size_second = field.shape[1]
    offset = 1 if layout == "both" else 0
    start = 0 if sense == 1 else 2
    if along == 0:
        return padded[start : start + size_first, offset : offset + size_second]
    return padded[1 : 1 + size_first, start : start + size_second]


def incoming_weights(coeffs, layout):
    size_first = coeffs.shape[1]
    size_second = coeffs.shape[2]
    if layout == "both":
        padded = with_halo(coeffs[0:4], (("blk", 1), ("grp", 2)), 1)
        return (
            padded[0, 0:size_first, 1 : size_second + 1],
            padded[1, 2 : size_first + 2, 1 : size_second + 1],
            padded[2, 1 : size_first + 1, 0:size_second],
            padded[3, 1 : size_first + 1, 2 : size_second + 2],
        )
    padded = with_halo(coeffs[0:2], (("blk", 1),), 1)
    return (padded[0, 0:size_first], padded[1, 2 : size_first + 2])


def shared_dims(layout):
    if layout == "both":
        return (0, 1)
    return (0,)


def transposed(field, section):
    coeffs, centre, layout, incoming = section
    shared = shared_dims(layout)
    result = centre * field
    padded = spread_field(field, layout)
    for index in range(6):
        along, sense = DIRECTIONS[index]
        if along in shared:
            term = incoming[index] * neighbour(padded, along, sense, layout, field)
        else:
            term = moved(coeffs[index] * field, along, sense)
        result = result - term
    return result


def sweep(field, source, section):
    return field + relaxation * (source - transposed(field, section)) / section[1]


def build_sections(weights):
    sections = []
    coeffs = weights
    for level in range(LEVELS):
        if level > 0:
            coeffs = restrict(coeffs) * 0.25
        layout = "both" if level < LEVELS - 2 else "blk"
        if level == LEVELS - 2:
            coeffs = lax.all_gather(coeffs, "grp", axis=2, tiled=True)
        incoming = ()
        incoming = incoming_weights(coeffs, layout)
        sections.append((coeffs, jnp.sum(coeffs, axis=0), layout, incoming))
    return sections


def coarse_solve(source, section):
    field = relaxation * source / section[1]
    for count in range(COARSE_SWEEPS - 1):
        field = sweep(field, source, section)
    return field


def vcycle(level, source, sections):
    section = sections[level]
    if level == LEVELS - 1:
        return coarse_solve(source, section)
    field = relaxation * source / section[1]
    field = sweep(field, source, section)
    coarse = restrict(source - transposed(field, section))
    rows = coarse.shape[1]
    if level == LEVELS - 3:
        coarse = lax.all_gather(coarse, "grp", axis=1, tiled=True)
    correction = vcycle(level + 1, coarse, sections)
    if level == LEVELS - 3:
        correction = lax.dynamic_slice_in_dim(correction, lax.axis_index("grp") * rows, rows, 1)
    field = field + prolong(correction)
    for count in range(SWEEPS):
        field = sweep(field, source, section)
    return field


def body(right_side, weights):
    sections = build_sections(weights)
    solution_field = vcycle(0, right_side, sections)
    update = right_side - transposed(solution_field, sections[0])
    solution_field = solution_field + vcycle(0, update, sections)
    residual = right_side - transposed(solution_field, sections[0])
    return (solution_field, residual)


def solution(mesh):
    return jax.shard_map(
        body,
        mesh=mesh,
        in_specs=(P("blk", "grp", None), P(None, "blk", "grp", None)),
        out_specs=(P("blk", "grp", None), P("blk", "grp", None)),
        check_vma=False,
    )
```

profile of v0, /device:TPU:104, one launch (start us, length us, event | category | flops | bytes accessed | tf_op | source)
XLA Modules:
  0.0 965.2 jit_solution(298580264673193761)
XLA Ops:
  3.8 4.5 collective-permute-start.3
  14.6 18.0 %copy.876 = f32[6,16,16,256]{0,3,2,1:T(8,128)} copy(f32[6,16,16,256]{3,2,1,0:T(8,128)} %param.3) | data formatting | bytes 3145728 | tf_op args[1]
  32.6 24.3 %reduce_sum.178 = f32[6,8,8,128]{0,3,2,1:T(8,128)} reduce(f32[6,8,2,8,2,128,2]{0,6,5,4,3,2,1:T(2,128)} %bitcast.559, f32[]{:T(128)} %constant.24.clone.1), dimensions={2,4,6}, to_apply=%region_2.0 | reduce | flops 344064 | bytes 1769476 | tf_op jit(solution)/shard_map/reduce_sum | solution.py:48
  56.8 5.2 broadcast_multiply_fusion
  62.0 4.8 reduce_sum.181
  68.4 5.1 collective-permute-start.26
  78.9 4.4 slice_reduce_fusion.1
  83.7 13.1 %all_gather.10 = f32[6,2,16,32]{3,1,0,2:T(2,128)S(1)} all-gather(f32[6,2,2,32]{3,1,0,2:T(2,128)S(1)} %copy.895), channel_id=1, replica_groups=mesh['blk'=16,'grp'=8] {'grp'}, dimensions={2}, use_global_device_ids=true | all-gather | bytes 27648 | tf_op jit(solution)/shard_map/all_gather | solution.py:121
  105.5 6.0 collective-permute-start.2
  148.2 4.7 collective-permute-start.9
  177.7 18.1 %reshape.318 = f32[8,2,8,2,128,2]{5,4,3,2,1,0:T(8,128)} reshape(f32[16,16,256]{2,1,0:T(8,128)S(1)} %fusion.110) | data formatting | bytes 524288 | tf_op jit(solution)/shard_map/reshape | solution.py:47
  195.8 7.6 reduce_sum.177
  204.3 6.0 collective-permute-start.15
  212.5 10.8 %fusion.1 = (f32[8,8,128]{2,1,0:T(8,128)S(1)}, f32[8,8,128]{2,1,0:T(8,128)S(1)}) fusion(f32[4,10,1,128]{0,3,2,1:T(8,128)} %copy.882, f32[4,1,8,128]{0,3,2,1:T(8,128)S(1)} %copy-done.5, f32[4,8,8,128]{0,3,2,1:T(8,128)} %bitcast.558, f32[4,1,8,128]{0,3,2,1:T(8,128)} %copy-done.6, f32[4,10,1,128]{0,3,2,1:T(8,128)} %copy.884), kind=kLoop, calls=%fused_computation.7 | loop fusion | flops 49152 | bytes 270336 | tf_op jit(solution)/shard_map/slice | solution.py:81
  230.4 6.0 collective-permute-start.21
  243.6 6.0 collective-permute-start.38
  268.7 3.9 collective-permute-start.25
  300.1 11.6 %all_gather.9 = f32[2,16,32]{2,0,1:T(2,128)S(1)} all-gather(f32[2,2,32]{2,0,1:T(2,128)S(1)} %copy.893), channel_id=1, replica_groups=mesh['blk'=16,'grp'=8] {'grp'}, dimensions={1}, use_global_device_ids=true | all-gather | bytes 4608 | tf_op jit(solution)/shard_map/all_gather | solution.py:144
  313.6 3.9 collective-permute-start.37
  322.3 4.5 collective-permute-start.41
  328.7 5.7 collective-permute-done.40
  336.7 3.9 collective-permute-start.43
  346.3 3.9 collective-permute-start.46
  355.9 3.9 collective-permute-start.48
  365.5 3.9 collective-permute-start.50
  375.1 3.9 collective-permute-start.52
  384.7 3.9 collective-permute-start.54
  394.3 3.9 collective-permute-start.56
  404.3 3.9 collective-permute-start.58
  414.1 3.9 collective-permute-start.60
  424.2 3.9 collective-permute-start.62
  441.0 3.9 collective-permute-start.66
  462.0 3.9 collective-permute-start.70
  478.5 3.9 collective-permute-start.74
  493.1 6.4 broadcast_in_dim.66
  499.5 12.7 %reshape.324 = f32[16,16,256]{2,1,0:T(8,128)S(1)} reshape(f32[8,2,8,2,128,2]{5,4,3,2,1,0:T(8,128)} %broadcast_in_dim.66) | data formatting | bytes 524288 | tf_op jit(solution)/shard_map/reshape | solution.py:54
  514.2 3.9 collective-permute-start.78
  531.2 3.9 collective-permute-start.82
  548.2 3.9 collective-permute-start.86
  565.2 3.9 collective-permute-start.90
  582.3 3.9 collective-permute-start.94
  597.3 18.1 %reshape.325 = f32[8,2,8,2,128,2]{5,4,3,2,1,0:T(8,128)} reshape(f32[16,16,256]{2,1,0:T(8,128)S(1)} %fusion.46) | data formatting | bytes 524288 | tf_op jit(solution)/shard_map/reshape | solution.py:47
  615.4 7.0 reduce_sum.194
  624.4 3.9 collective-permute-start.98
  641.0 3.9 collective-permute-start.102
  662.8 3.9 collective-permute-start.106
  679.3 3.9 collective-permute-start.110
  695.5 11.0 %all_gather.11 = f32[2,16,32]{2,0,1:T(2,128)S(1)} all-gather(f32[2,2,32]{2,0,1:T(2,128)S(1)} %copy.907), channel_id=1, replica_groups=mesh['blk'=16,'grp'=8] {'grp'}, dimensions={1}, use_global_device_ids=true | all-gather | bytes 4608 | tf_op jit(solution)/shard_map/all_gather | solution.py:144
  708.5 3.9 collective-permute-start.114
  719.1 3.9 collective-permute-start.116
  729.7 3.9 collective-permute-start.118
  740.0 3.9 collective-permute-start.120
  750.3 3.9 collective-permute-start.122
  760.6 3.9 collective-permute-start.124
  770.9 3.9 collective-permute-start.126
  781.2 3.9 collective-permute-start.128
  791.5 3.9 collective-permute-start.130
  802.1 3.9 collective-permute-start.132
  812.6 3.9 collective-permute-start.134
  824.1 3.9 collective-permute-start.136
  841.3 3.9 collective-permute-start.140
  863.0 3.9 collective-permute-start.144
  894.1 6.4 broadcast_in_dim.73
  900.5 12.7 %reshape.330 = f32[16,16,256]{2,1,0:T(8,128)S(1)} reshape(f32[8,2,8,2,128,2]{5,4,3,2,1,0:T(8,128)} %broadcast_in_dim.73) | data formatting | bytes 524288 | tf_op jit(solution)/shard_map/reshape | solution.py:54
  (659 shorter events, 571.2 us)
Async XLA Ops:
  3.8 110.6 %collective-permute-start.3 = (f32[1,16,256]{2,1,0:T(8,128)}, f32[1,16,256]{2,1,0:T(8,128)}, u32[]{:S(2)}, u32[]{:S(2)}) collective-permute-start(f32[1,16,256]{2,1,0:T(8,128)} %get-tuple-element.131), channel_id=1, source_target_pairs={{8,0},{16,8},{24,16},{32,24},{40,32},{48,40},{56,48},{64,56},{72,6... | collective-permute-start | bytes 49160 | tf_op jit(solution)/shard_map/ppermute | solution.py:25
  8.3 110.0 %collective-permute-start.1 = (f32[1,16,256]{2,1,0:T(8,128)}, f32[1,16,256]{2,1,0:T(8,128)}, u32[]{:S(2)}, u32[]{:S(2)}) collective-permute-start(f32[1,16,256]{2,1,0:T(8,128)} %get-tuple-element.130), channel_id=1, source_target_pairs={{0,8},{8,16},{16,24},{24,32},{32,40},{40,48},{48,56},{56,64},{64,7... | collective-permute-start | bytes 49160 | tf_op jit(solution)/shard_map/ppermute | solution.py:23
  11.8 109.9 %collective-permute-start = (f32[4,1,16,256]{3,2,1,0:T(8,128)}, f32[4,1,16,256]{3,2,1,0:T(8,128)}, u32[]{:S(2)}, u32[]{:S(2)}) collective-permute-start(f32[4,1,16,256]{3,2,1,0:T(8,128)} %get-tuple-element.61), channel_id=1, source_target_pairs={{0,8},{8,16},{16,24},{24,32},{32,40},{40,48},{48,56},{56,64},{64,7... | collective-permute-start | bytes 196616 | tf_op jit(solution)/shard_map/ppermute | solution.py:23
  68.4 37.1 %collective-permute-start.26 = (f32[4,1,4,64]{0,3,2,1:T(8,128)}, f32[4,1,4,64]{0,3,2,1:T(8,128)S(1)}, u32[]{:S(2)}, u32[]{:S(2)}) collective-permute-start(f32[4,1,4,64]{0,3,2,1:T(8,128)} %get-tuple-element.69), channel_id=1, source_target_pairs={{8,0},{16,8},{24,16},{32,24},{40,32},{48,40},{56,48},{64,56},{72,6... | collective-permute-start | bytes 12296 | tf_op jit(solution)/shard_map/ppermute | solution.py:25
  73.6 38.0 %collective-permute-start.24 = (f32[4,1,4,64]{0,3,2,1:T(8,128)}, f32[4,1,4,64]{0,3,2,1:T(8,128)S(1)}, u32[]{:S(2)}, u32[]{:S(2)}) collective-permute-start(f32[4,1,4,64]{0,3,2,1:T(8,128)} %get-tuple-element.68), channel_id=1, source_target_pairs={{0,8},{8,16},{16,24},{24,32},{32,40},{40,48},{48,56},{56,64},{64,7... | collective-permute-start | bytes 12296 | tf_op jit(solution)/shard_map/ppermute | solution.py:23
  105.5 18.1 %collective-permute-start.2 = (f32[4,1,16,256]{3,2,1,0:T(8,128)S(1)}, f32[4,1,16,256]{3,2,1,0:T(8,128)S(1)}, u32[]{:S(2)}, u32[]{:S(2)}) collective-permute-start(f32[4,1,16,256]{3,2,1,0:T(8,128)S(1)} %copy-done.45), channel_id=1, source_target_pairs={{8,0},{16,8},{24,16},{32,24},{40,32},{48,40},{56,48},{64,56},{72,6... | collective-permute-start | bytes 196616 | tf_op jit(solution)/shard_map/ppermute | solution.py:25
  111.5 16.0 %collective-permute-start.14 = (f32[4,1,8,128]{0,3,2,1:T(8,128)}, f32[4,1,8,128]{0,3,2,1:T(8,128)S(1)}, u32[]{:S(2)}, u32[]{:S(2)}) collective-permute-start(f32[4,1,8,128]{0,3,2,1:T(8,128)} %get-tuple-element.57), channel_id=1, source_target_pairs={{8,0},{16,8},{24,16},{32,24},{40,32},{48,40},{56,48},{64,56},{72,6... | collective-permute-start | bytes 49160 | tf_op jit(solution)/shard_map/ppermute | solution.py:25
  114.4 18.3 %collective-permute-start.12 = (f32[4,1,8,128]{0,3,2,1:T(8,128)}, f32[4,1,8,128]{0,3,2,1:T(8,128)S(1)}, u32[]{:S(2)}, u32[]{:S(2)}) collective-permute-start(f32[4,1,8,128]{0,3,2,1:T(8,128)} %get-tuple-element.56), channel_id=1, source_target_pairs={{0,8},{8,16},{16,24},{24,32},{32,40},{40,48},{48,56},{56,64},{64,7... | collective-permute-start | bytes 49160 | tf_op jit(solution)/shard_map/ppermute | solution.py:23
  118.4 199.4 %collective-permute-start.36 = (f32[2,1,16,32]{3,1,2,0:T(1,128)}, f32[2,1,16,32]{3,1,2,0:T(1,128)}, u32[]{:S(2)}, u32[]{:S(2)}) collective-permute-start(f32[2,1,16,32]{3,1,2,0:T(1,128)} %copy.910), channel_id=1, source_target_pairs={{0,8},{8,16},{16,24},{24,32},{32,40},{40,48},{48,56},{56,64},{64,7... | collective-permute-start | bytes 12296 | tf_op jit(solution)/shard_map/ppermute | solution.py:23
  121.7 19.2 %collective-permute-start.7 = (f32[18,1,256]{2,1,0:T(1,128)}, f32[18,1,256]{2,1,0:T(1,128)S(1)}, u32[]{:S(2)}, u32[]{:S(2)}) collective-permute-start(f32[18,1,256]{2,1,0:T(1,128)} %get-tuple-element.91), channel_id=1, source_target_pairs={{1,0},{2,1},{3,2},{4,3},{5,4},{6,5},{7,6},{9,8},{10,9},{11,10},{12... | collective-permute-start | bytes 55304 | tf_op jit(solution)/shard_map/ppermute | solution.py:25
  123.6 19.6 %collective-permute-start.5 = (f32[18,1,256]{2,1,0:T(1,128)}, f32[18,1,256]{2,1,0:T(1,128)S(1)}, u32[]{:S(2)}, u32[]{:S(2)}) collective-permute-start(f32[18,1,256]{2,1,0:T(1,128)} %get-tuple-element.90), channel_id=1, source_target_pairs={{0,1},{1,2},{2,3},{3,4},{4,5},{5,6},{6,7},{8,9},{9,10},{10,11},{11... | collective-permute-start | bytes 55304 | tf_op jit(solution)/shard_map/ppermute | solution.py:23
  127.6 18.9 %collective-permute-start.4 = (f32[4,18,1,256]{3,2,1,0:T(1,128)}, f32[4,18,1,256]{3,2,1,0:T(1,128)}, u32[]{:S(2)}, u32[]{:S(2)}) collective-permute-start(f32[4,18,1,256]{3,2,1,0:T(1,128)} %get-tuple-element.65), channel_id=1, source_target_pairs={{0,1},{1,2},{2,3},{3,4},{4,5},{5,6},{6,7},{8,9},{9,10},{10,11},{11... | collective-permute-start | bytes 221192 | tf_op jit(solution)/shard_map/ppermute | solution.py:23
  132.7 13.8 %collective-permute-start.6 = (f32[4,18,1,256]{3,2,1,0:T(1,128)S(1)}, f32[4,18,1,256]{3,2,1,0:T(1,128)}, u32[]{:S(2)}, u32[]{:S(2)}) collective-permute-start(f32[4,18,1,256]{3,2,1,0:T(1,128)S(1)} %get-tuple-element.64), channel_id=1, source_target_pairs={{1,0},{2,1},{3,2},{4,3},{5,4},{6,5},{7,6},{9,8},{10,9},{11,10},{12... | collective-permute-start | bytes 221192 | tf_op jit(solution)/shard_map/ppermute | solution.py:25
  140.9 19.5 %collective-permute-start.16 = (f32[4,10,1,128]{3,0,2,1:T(4,128)}, f32[4,10,1,128]{3,0,2,1:T(4,128)}, u32[]{:S(2)}, u32[]{:S(2)}) collective-permute-start(f32[4,10,1,128]{3,0,2,1:T(4,128)} %copy.881), channel_id=1, source_target_pairs={{0,1},{1,2},{2,3},{3,4},{4,5},{5,6},{6,7},{8,9},{9,10},{10,11},{11... | collective-permute-start | bytes 61448 | tf_op jit(solution)/shard_map/ppermute | solution.py:23
  143.3 20.9 %collective-permute-start.18 = (f32[4,10,1,128]{3,0,2,1:T(4,128)}, f32[4,10,1,128]{3,0,2,1:T(4,128)}, u32[]{:S(2)}, u32[]{:S(2)}) collective-permute-start(f32[4,10,1,128]{3,0,2,1:T(4,128)} %copy.883), channel_id=1, source_target_pairs={{1,0},{2,1},{3,2},{4,3},{5,4},{6,5},{7,6},{9,8},{10,9},{11,10},{12... | collective-permute-start | bytes 61448 | tf_op jit(solution)/shard_map/ppermute | solution.py:25
  148.2 21.4 %collective-permute-start.9 = (f32[1,16,256]{2,1,0:T(8,128)S(1)}, f32[1,16,256]{2,1,0:T(8,128)S(1)}, u32[]{:S(2)}, u32[]{:S(2)}) collective-permute-start(f32[1,16,256]{2,1,0:T(8,128)S(1)} %get-tuple-element.127), channel_id=1, source_target_pairs={{8,0},{16,8},{24,16},{32,24},{40,32},{48,40},{56,48},{64,56},{72,6... | collective-permute-start | bytes 49160 | tf_op jit(solution)/shard_map/ppermute | solution.py:25
  153.0 16.7 %collective-permute-start.8 = (f32[1,16,256]{2,1,0:T(8,128)S(1)}, f32[1,16,256]{2,1,0:T(8,128)S(1)}, u32[]{:S(2)}, u32[]{:S(2)}) collective-permute-start(f32[1,16,256]{2,1,0:T(8,128)S(1)} %get-tuple-element.126), channel_id=1, source_target_pairs={{0,8},{8,16},{16,24},{24,32},{32,40},{40,48},{48,56},{56,64},{64,7... | collective-permute-start | bytes 49160 | tf_op jit(solution)/shard_map/ppermute | solution.py:23
  160.4 83.2 %collective-permute-start.28 = (f32[4,6,1,64]{0,3,2,1:T(8,128)}, f32[4,6,1,64]{0,3,2,1:T(8,128)}, u32[]{:S(2)}, u32[]{:S(2)}) collective-permute-start(f32[4,6,1,64]{0,3,2,1:T(8,128)} %get-tuple-element.66), channel_id=1, source_target_pairs={{0,1},{1,2},{2,3},{3,4},{4,5},{5,6},{6,7},{8,9},{9,10},{10,11},{11... | collective-permute-start | bytes 18440 | tf_op jit(solution)/shard_map/ppermute | solution.py:23
  164.1 86.5 %collective-permute-start.30 = (f32[4,6,1,64]{0,3,2,1:T(8,128)}, f32[4,6,1,64]{0,3,2,1:T(8,128)}, u32[]{:S(2)}, u32[]{:S(2)}) collective-permute-start(f32[4,6,1,64]{0,3,2,1:T(8,128)} %get-tuple-element.67), channel_id=1, source_target_pairs={{1,0},{2,1},{3,2},{4,3},{5,4},{6,5},{7,6},{9,8},{10,9},{11,10},{12... | collective-permute-start | bytes 18440 | tf_op jit(solution)/shard_map/ppermute | solution.py:25
  204.3 19.0 %collective-permute-start.15 = (f32[1,8,128]{2,1,0:T(8,128)S(1)}, f32[1,8,128]{2,1,0:T(8,128)S(1)}, u32[]{:S(2)}, u32[]{:S(2)}) collective-permute-start(f32[1,8,128]{2,1,0:T(8,128)S(1)} %get-tuple-element.187), channel_id=1, source_target_pairs={{8,0},{16,8},{24,16},{32,24},{40,32},{48,40},{56,48},{64,56},{72,6... | collective-permute-start | bytes 12296 | tf_op jit(solution)/shard_map/ppermute | solution.py:25
  210.4 13.0 %collective-permute-start.13 = (f32[1,8,128]{2,1,0:T(8,128)S(1)}, f32[1,8,128]{2,1,0:T(8,128)S(1)}, u32[]{:S(2)}, u32[]{:S(2)}) collective-permute-start(f32[1,8,128]{2,1,0:T(8,128)S(1)} %get-tuple-element.186), channel_id=1, source_target_pairs={{0,8},{8,16},{16,24},{24,32},{32,40},{40,48},{48,56},{56,64},{64,7... | collective-permute-start | bytes 12296 | tf_op jit(solution)/shard_map/ppermute | solution.py:23
  230.4 23.3 %collective-permute-start.21 = (f32[1,8,128]{2,1,0:T(8,128)S(1)}, f32[1,8,128]{2,1,0:T(8,128)S(1)}, u32[]{:S(2)}, u32[]{:S(2)}) collective-permute-start(f32[1,8,128]{2,1,0:T(8,128)S(1)} %get-tuple-element.183), channel_id=1, source_target_pairs={{8,0},{16,8},{24,16},{32,24},{40,32},{48,40},{56,48},{64,56},{72,6... | collective-permute-start | bytes 12296 | tf_op jit(solution)/shard_map/ppermute | solution.py:25
  236.4 17.2 %collective-permute-start.20 = (f32[1,8,128]{2,1,0:T(8,128)S(1)}, f32[1,8,128]{2,1,0:T(8,128)S(1)}, u32[]{:S(2)}, u32[]{:S(2)}) collective-permute-start(f32[1,8,128]{2,1,0:T(8,128)S(1)} %get-tuple-element.182), channel_id=1, source_target_pairs={{0,8},{8,16},{16,24},{24,32},{32,40},{40,48},{48,56},{56,64},{64,7... | collective-permute-start | bytes 12296 | tf_op jit(solution)/shard_map/ppermute | solution.py:23
  243.6 76.1 %collective-permute-start.38 = (f32[2,1,16,32]{3,1,2,0:T(1,128)S(1)}, f32[2,1,16,32]{3,1,2,0:T(1,128)S(1)}, u32[]{:S(2)}, u32[]{:S(2)}) collective-permute-start(f32[2,1,16,32]{3,1,2,0:T(1,128)S(1)} %copy.912), channel_id=1, source_target_pairs={{8,0},{16,8},{24,16},{32,24},{40,32},{48,40},{56,48},{64,56},{72,6... | collective-permute-start | bytes 12296 | tf_op jit(solution)/shard_map/ppermute | solution.py:25
  250.7 90.0 %collective-permute-start.44 = (f32[2,1,8,16]{3,2,0,1:T(8,128)}, f32[2,1,8,16]{3,2,0,1:T(8,128)S(1)}, u32[]{:S(2)}, u32[]{:S(2)}) collective-permute-start(f32[2,1,8,16]{3,2,0,1:T(8,128)} %slice_bitcast_fusion.6), channel_id=1, source_target_pairs={{8,0},{16,8},{24,16},{32,24},{40,32},{48,40},{56,48},{64,56},{72,6... | collective-permute-start | bytes 3080 | tf_op jit(solution)/shard_map/ppermute | solution.py:25
  268.7 7.6 collective-permute-start.25
  311.7 8.0 collective-permute-start.39
  313.6 7.7 collective-permute-start.37
  317.7 23.0 %collective-permute-start.42 = (f32[2,1,8,16]{3,2,0,1:T(8,128)S(1)}, f32[2,1,8,16]{3,2,0,1:T(8,128)S(1)}, u32[]{:S(2)}, u32[]{:S(2)}) collective-permute-start(f32[2,1,8,16]{3,2,0,1:T(8,128)S(1)} %copy-done.48), channel_id=1, source_target_pairs={{0,8},{8,16},{16,24},{24,32},{32,40},{40,48},{48,56},{56,64},{64,7... | collective-permute-start | bytes 3080 | tf_op jit(solution)/shard_map/ppermute | solution.py:23
  326.8 7.7 collective-permute-start.40
  336.7 7.6 collective-permute-start.43
  346.3 7.6 collective-permute-start.46
  355.9 7.6 collective-permute-start.48
  365.5 7.6 collective-permute-start.50
  375.1 7.6 collective-permute-start.52
  384.7 7.6 collective-permute-start.54
  394.3 7.6 collective-permute-start.56
  404.3 7.7 collective-permute-start.58
  414.1 7.7 collective-permute-start.60
  462.0 7.6 collective-permute-start.70
  478.5 7.6 collective-permute-start.74
  514.2 7.7 collective-permute-start.78
  531.2 7.7 collective-permute-start.82
  548.2 7.7 collective-permute-start.86
  565.2 7.7 collective-permute-start.90
  582.3 7.7 collective-permute-start.94
  624.4 7.6 collective-permute-start.98
  641.0 7.6 collective-permute-start.102
  708.5 7.7 collective-permute-start.114
  719.1 7.7 collective-permute-start.116
  729.7 7.6 collective-permute-start.118
  740.0 7.6 collective-permute-start.120
  750.3 7.6 collective-permute-start.122
  760.6 7.6 collective-permute-start.124
  770.9 7.6 collective-permute-start.126
  781.2 7.6 collective-permute-start.128
  791.5 7.6 collective-permute-start.130
  802.1 7.7 collective-permute-start.132
  812.6 7.7 collective-permute-start.134
  863.0 7.6 collective-permute-start.144
  879.5 7.6 collective-permute-start.148
  915.2 7.7 collective-permute-start.152
  932.2 7.7 collective-permute-start.156
  949.3 7.7 collective-permute-start.160
  (149 other events, 3498.4 us)
where the time goes:
time: 980 us; the launch traced here: 965 us
  starting transfers between devices  449 us (46%)
  waiting for transfers between devices  221 us (23%)
  local copies, waits for them, and re-layouts  150 us (15%)
  other arithmetic  105 us (11%)
  blocking collectives  35.7 us (4%)
    ppermute x82, starting transfers between devices, with_halo(): lax.ppermute(tail, axis, [(i, (i + 1) % count) for i in range(ends)])  261 us
    ppermute x82, waiting for transfers between devices, with_halo(): lax.ppermute(tail, axis, [(i, (i + 1) % count) for i in range(ends)])  221 us
    ppermute x82, starting transfers between devices, with_halo(): lax.ppermute(head, axis, [((i + 1) % count, i) for i in range(ends)])  188 us
    reduce_sum x15, other arithmetic, restrict(): return blocks.mean(axis=(-5, -3, -1))  49.4 us
    reshape x6, local copies, waits for them, and re-layouts, restrict(): array.reshape(lead + (shape[-3] // 2, 2, shape[-2] // 2, 2, shape[-1] //...  44.3 us
    reshape x6, local copies, waits for them, and re-layouts, prolong(): return wide.reshape(depth * 2, height * 2, width * 2)  31.2 us
    all_gather x2, blocking collectives, vcycle(): coarse = lax.all_gather(coarse, 'grp', axis=1, tiled=True)  22.6 us
  transfers between devices with their start and end apart: 164, of which 70 were waited for; matrix products, arithmetic and copies ran while one was open for 16% of the time, Pallas kernels for 0%

commit v1 on v0

v1 whole, which is shorter than its diff:
```python
import functools

import jax
import jax.numpy as jnp
from jax import lax
from jax.experimental import pallas as pl
from jax.experimental.pallas import tpu as pltpu
from jax.sharding import PartitionSpec as P

MESH = pl.DeviceIdType.MESH
F32 = jnp.float32
BLK, GRP = 16, 8
OMEGA = 0.7
KEEP = 1.0 - OMEGA
NEIGHBOURS = tuple((dx, dy) for dx in (-1, 0, 1) for dy in (-1, 0, 1) if (dx, dy) != (0, 0))
CYCLES = 2


def lane_roll(v, n):
    return pltpu.roll(v, n % 128, v.ndim - 1)


def row_roll(v, n):
    axis = v.ndim - 2
    return pltpu.roll(v, n % v.shape[axis], axis)


def lane_index(shape):
    return lax.broadcasted_iota(jnp.int32, shape, len(shape) - 1)


def lane_swap(v, n):
    even = lax.rem(lax.div(lane_index(v.shape), n), 2) == 0
    return jnp.where(even, lane_roll(v, -n), lane_roll(v, n))


def split_dot(x, matrix):
    high = x.astype(jnp.bfloat16)
    rest = x - high.astype(F32)
    middle = rest.astype(jnp.bfloat16)
    low = (rest - middle.astype(F32)).astype(jnp.bfloat16)
    dot = functools.partial(jnp.dot, preferred_element_type=F32)
    return (dot(low, matrix) + dot(middle, matrix)) + dot(high, matrix)


def span(delta, size, halo, start):
    if delta == 1:
        return pl.ds(start + size - halo, halo), pl.ds(start - halo, halo)
    if delta == -1:
        return pl.ds(start, halo), pl.ds(start + size, halo)
    return pl.ds(start, size), pl.ds(start, size)


def kernel(
    rhs_ref, w_ref, sol_ref, res_ref,
    w0, f0, rc0, cr0, g0, big0, a0, b0, x0, s0,
    w1, f1, rc1, cr1, g1, big1, a1, b1, t1,
    w2, f2, rc2, cr2, g2, x2, big2, a2, b2, t2,
    w3row, w3, f3, rc3, cr3, g3row, g3, c3, t3,
    f4, rc4, tmp, dummy6, dummy1,
    send_sem, recv_sem, all_send, all_recv,
):
    b = lax.axis_index("blk")
    g = lax.axis_index("grp")

    def device(dx, dy):
        return (lax.rem(b + dx + BLK, BLK), lax.rem(g + dy + GRP, GRP))

    barrier = pltpu.get_barrier_semaphore()

    def greet(k, carry):
        pl.semaphore_signal(
            barrier, inc=1, device_id=device(lax.div(k, GRP), lax.rem(k, GRP)), device_id_type=MESH
        )
        return carry

    lax.fori_loop(1, BLK * GRP, greet, 0)

    def loop(begin, end, step):
        def one(index, carry):
            step(index)
            return carry

        lax.fori_loop(begin, end, one, 0)

    def copies(view, lead, size, halo, start_x, start_y, slot):
        out = []
        for n, (dx, dy) in enumerate(NEIGHBOURS):
            sx, tx = span(dx, size, halo, start_x)
            sy, ty = span(dy, size, halo, start_y)
            out.append(
                pltpu.make_async_remote_copy(
                    src_ref=view.at[lead + (sx, sy)],
                    dst_ref=view.at[lead + (tx, ty)],
                    send_sem=send_sem.at[slot, n],
                    recv_sem=recv_sem.at[slot, n],
                    device_id=device(dx, dy),
                    device_id_type=MESH,
                )
            )
        return out

    pending = []

    def start(batch):
        for copy in batch:
            copy.start()
        pending.extend(batch)

    def arrived(batch):
        for copy in batch:
            copy.wait_recv()

    def spread_all(row, gathered, slot):
        mine = pltpu.make_async_copy(row, gathered.at[:, b, pl.ds(g, 1), :], all_recv.at[slot])
        mine.start()

        def send(k, carry):
            pltpu.make_async_remote_copy(
                src_ref=row,
                dst_ref=gathered.at[:, b, pl.ds(g, 1), :],
                send_sem=all_send.at[slot],
                recv_sem=all_recv.at[slot],
                device_id=device(lax.div(k, GRP), lax.rem(k, GRP)),
                device_id_type=MESH,
            ).start()
            return carry

        lax.fori_loop(1, BLK * GRP, send, 0)

    def gathered_all(gathered, slot):
        pltpu.make_async_copy(gathered, gathered, all_recv.at[slot]).wait()

    def sent_all(dummy, slot):
        pltpu.make_async_copy(dummy, dummy, all_send.at[slot]).wait()

    def inside(rows, size, start_x, start_y):
        row = lax.broadcasted_iota(jnp.int32, (rows, 128), 0) + (g * size - start_y)

        def mask(plane):
            x = b * size + plane - start_x
            ok = jnp.logical_and(x >= 0, x < BLK * size)
            shifted = row + jnp.where(ok, 0, 1 << 20)
            return jnp.logical_and(shifted >= 0, shifted < GRP * size)

        return mask

    zi = lax.broadcasted_iota(jnp.int32, (256, 256), 0)
    ci = lax.broadcasted_iota(jnp.int32, (256, 256), 1)
    parted = jnp.where(ci < 128, 2 * ci, 2 * ci - 255)
    split = jnp.where(zi == parted, 1.0, 0.0).astype(jnp.bfloat16)
    parts = split_dot(rhs_ref[...].reshape(256, 256), split)
    g0[0, 0, 4:20, 4:20, :] = parts[:, :128].reshape(16, 16, 128)
    g0[0, 1, 4:20, 4:20, :] = parts[:, 128:].reshape(16, 16, 128)

    def part_weights(k):
        both = split_dot(w_ref[k].reshape(256, 256), split)
        w0[2 * k, 4:20, 4:20, :] = both[:, :128].reshape(16, 16, 128)
        w0[2 * k + 1, 4:20, 4:20, :] = both[:, 128:].reshape(16, 16, 128)

    loop(0, 6, part_weights)

    pl.semaphore_wait(barrier, BLK * GRP - 1)

    all_of = slice(None)
    w0_halo = copies(w0, (all_of,), 16, 3, 4, 4, 0)
    g0_halo = [copies(g0, (c, all_of), 16, 2, 4, 4, 3 + c) for c in range(CYCLES)]
    x0_halo = [copies(x0, (c, all_of), 16, 3, 4, 4, 5 + c) for c in range(CYCLES)]
    w1_halo = copies(w1, (all_of,), 8, 6, 6, 8, 1)
    g1_halo = [copies(g1, (c,), 8, 6, 6, 8, 7 + c) for c in range(CYCLES)]
    w2_halo = copies(w2, (all_of,), 4, 4, 4, 4, 2)
    x2_halo = [copies(x2, (c, all_of), 4, 4, 4, 4, 9 + c) for c in range(CYCLES)]

    start(g0_halo[0])
    start(w0_halo)

    def weights_1(i):
        for k in range(6):
            total = None
            for part in range(2):
                for dx in range(2):
                    for dy in range(2):
                        term = w0[2 * k + part, 4 + 2 * i + dx, pl.ds(4 + dy, 8, stride=2), :]
                        total = term if total is None else total + term
            w1[k, 6 + i, 8:16, :] = total * (1.0 / 32.0)

    loop(0, 8, weights_1)
    start(w1_halo)

    def weights_2(i):
        for k in range(6):
            total = None
            for dx in range(2):
                for dy in range(2):
                    term = w1[k, 6 + 2 * i + dx, pl.ds(8 + dy, 4, stride=2), :]
                    total = term if total is None else total + term
            w2[k, 4 + i, 4:8, :] = (total + lane_swap(total, 1)) * (1.0 / 32.0)

    loop(0, 4, weights_2)
    start(w2_halo)

    quad = lax.rem(lane_index((1, 128)), 4)

    def pack_quads(cells):
        out = cells[3]
        for n in range(3):
            out = jnp.where(quad == n, cells[n], out)
        return out

    def weights_3(k):
        cells = []
        for xl in range(2):
            for yl in range(2):
                total = None
                for dx in range(2):
                    for dy in range(2):
                        term = w2[k, 4 + 2 * xl + dx, pl.ds(4 + 2 * yl + dy, 1), :]
                        total = term if total is None else total + term
                cells.append((total + lane_swap(total, 2)) * (1.0 / 32.0))
        w3row[k] = pack_quads(cells)

    loop(0, 6, weights_3)
    spread_all(w3row, w3, 0)

    mask0 = inside(24, 16, 4, 4)
    mask1 = inside(24, 8, 6, 8)
    mask2 = inside(16, 4, 4, 4)
    lane24 = lane_index((24, 128))

    def relaxed(total, mask):
        return jnp.where(mask, OMEGA / total, 0.0)

    arrived(w0_halo)

    def fold_0(p):
        mask = mask0(p)
        rc = []
        for part in range(2):
            total = w0[part, p]
            for k in range(1, 6):
                total = total + w0[2 * k + part, p]
            rc.append(relaxed(total, mask))
            rc0[part, p] = rc[part]
            cr0[part, p] = total * (1.0 / OMEGA)
            f0[0 + part, p] = rc[part] * w0[0 + part, p - 1]
            f0[2 + part, p] = rc[part] * w0[2 + part, p + 1]
            f0[4 + part, p] = rc[part] * row_roll(w0[4 + part, p], 1)
            f0[6 + part, p] = rc[part] * row_roll(w0[6 + part, p], -1)
        f0[8, p] = rc[0] * jnp.where(lane24 == 0, 0.0, lane_roll(w0[9, p], 1))
        f0[9, p] = rc[1] * w0[8, p]
        f0[10, p] = rc[0] * w0[11, p]
        f0[11, p] = rc[1] * jnp.where(lane24 == 127, 0.0, lane_roll(w0[10, p], -1))

    loop(2, 22, fold_0)

    def sweep_0(u, p):
        e, o = u[0, p], u[1, p]
        out_e = KEEP * e + big0[0, p]
        out_o = KEEP * o + big0[1, p]
        out_e += f0[0, p] * u[0, p - 1]
        out_o += f0[1, p] * u[1, p - 1]
        out_e += f0[2, p] * u[0, p + 1]
        out_o += f0[3, p] * u[1, p + 1]
        out_e += f0[4, p] * row_roll(e, 1)
        out_o += f0[5, p] * row_roll(o, 1)
        out_e += f0[6, p] * row_roll(e, -1)
        out_o += f0[7, p] * row_roll(o, -1)
        out_e += f0[8, p] * lane_roll(o, 1)
        out_o += f0[9, p] * e
        out_e += f0[10, p] * o
        out_o += f0[11, p] * lane_roll(e, -1)
        return out_e, out_o

    def sweep_c(u, big, f, p, step):
        v = u[p]
        out = KEEP * v + big[p]
        out += f[0, p] * u[p - 1]
        out += f[1, p] * u[p + 1]
        out += f[2, p] * row_roll(v, 1)
        out += f[3, p] * row_roll(v, -1)
        out += f[4, p] * lane_roll(v, step)
        out += f[5, p] * lane_roll(v, -step)
        return out

    def fold_centre(w, rc, cr, p, mask):
        total = w[0, p]
        for k in range(1, 6):
            total = total + w[k, p]
        rc[p] = relaxed(total, mask)
        cr[p] = total * (1.0 / OMEGA)

    def fold_c(w, f, rc, p, step):
        r = rc[p]
        lanes = lane_index(r.shape)
        f[0, p] = r * w[0, p - 1]
        f[1, p] = r * w[1, p + 1]
        f[2, p] = r * row_roll(w[2, p], 1)
        f[3, p] = r * row_roll(w[3, p], -1)
        f[4, p] = r * jnp.where(lanes < step, 0.0, lane_roll(w[4, p], step))
        f[5, p] = r * jnp.where(lanes >= 128 - step, 0.0, lane_roll(w[5, p], -step))

    shape3 = (BLK, GRP, 128)

    def before(v):
        return jnp.concatenate([v[BLK - 1 :], v[: BLK - 1]], axis=0)

    def after(v):
        return jnp.concatenate([v[1:], v[:1]], axis=0)

    lane3 = lane_index(shape3)
    blk3 = lax.broadcasted_iota(jnp.int32, shape3, 0)
    grp3 = lax.broadcasted_iota(jnp.int32, shape3, 1)
    low_x = lax.rem(lax.div(lane3, 2), 2) == 0
    low_y = lax.rem(lane3, 2) == 0

    def shifts_3(v):
        r2, l2 = lane_roll(v, 2), lane_roll(v, -2)
        yield jnp.where(low_x, before(l2), r2)
        yield jnp.where(low_x, l2, after(r2))
        r1, l1 = lane_roll(v, 1), lane_roll(v, -1)
        yield jnp.where(low_y, row_roll(l1, 1), r1)
        yield jnp.where(low_y, l1, row_roll(r1, -1))
        yield lane_roll(v, 4)
        yield lane_roll(v, -4)

    def shifts_4(v):
        yield before(v)
        yield after(v)
        yield row_roll(v, 1)
        yield row_roll(v, -1)
        yield lane_roll(v, 8)
        yield lane_roll(v, -8)

    def octet(v):
        v = v + lane_swap(v, 1)
        v = v + lane_swap(v, 2)
        return v + lane_swap(v, 4)

    def fold_coarse():
        ws = [w3[k] for k in range(6)]
        total = ws[0] + ws[1] + ws[2] + ws[3] + ws[4] + ws[5]
        rc = OMEGA / total
        rc3[...] = rc
        cr3[...] = total * (1.0 / OMEGA)
        edge = (
            jnp.logical_and(blk3 == 0, low_x),
            jnp.logical_and(blk3 == BLK - 1, jnp.logical_not(low_x)),
            jnp.logical_and(grp3 == 0, low_y),
            jnp.logical_and(grp3 == GRP - 1, jnp.logical_not(low_y)),
            lane3 < 4,
            lane3 >= 124,
        )
        for k in range(6):
            moved = list(shifts_3(ws[k]))[k]
            f3[k] = jnp.where(edge[k], 0.0, rc * moved)
        total = None
        for k in range(6):
            coarse = octet(ws[k]) * (1.0 / 32.0)
            f4[k] = coarse
            total = coarse if total is None else total + coarse
        rc = OMEGA / total
        rc4[...] = rc
        edge = (blk3 == 0, blk3 == BLK - 1, grp3 == 0, grp3 == GRP - 1, lane3 < 8, lane3 >= 120)
        for k in range(6):
            moved = list(shifts_4(f4[k]))[k]
            f4[k] = jnp.where(edge[k], 0.0, rc * moved)

    def sweep_3(v, big):
        out = KEEP * v + big
        for k, moved in enumerate(shifts_3(v)):
            out += f3[k] * moved
        return out

    def sweep_4(v, big):
        out = KEEP * v + big
        for k, moved in enumerate(shifts_4(v)):
            out += f4[k] * moved
        return out

    def coarse_levels(source):
        big = rc3[...] * source
        u = sweep_3(big, big)
        left = (sweep_3(u, big) - u) * cr3[...]
        big_4 = rc4[...] * (octet(left) * 0.125)
        v = lax.fori_loop(0, 7, lambda n, v: sweep_4(v, big_4), big_4)
        u = u + v
        u = sweep_3(u, big)
        return sweep_3(u, big)

    for c in range(CYCLES):
        arrived(g0_halo[c])

        def source_0(p):
            for part in range(2):
                big0[part, p] = rc0[part, p] * g0[c, part, p]

        loop(2, 22, source_0)

        def down_0(p):
            a0[0, p], a0[1, p] = sweep_0(big0, p)

        loop(3, 21, down_0)

        def restrict_0(i):
            total = None
            for dx in range(2):
                p = 4 + 2 * i + dx
                e, o = sweep_0(a0, p)
                left = (e - a0[0, p]) * cr0[0, p] + (o - a0[1, p]) * cr0[1, p]
                total = left if total is None else total + left
            tmp[i] = total
            rows = tmp[i, pl.ds(4, 8, stride=2), :] + tmp[i, pl.ds(5, 8, stride=2), :]
            g1[c, 6 + i, 8:16, :] = rows * 0.125

        loop(0, 8, restrict_0)
        start(g1_halo[c])

        def keep_0(p):
            for part in range(2):
                x0[c, part, p, 4:20, :] = a0[part, p, 4:20, :]

        loop(4, 20, keep_0)
        start(x0_halo[c])

        if c == 0:
            arrived(w1_halo)
            loop(0, 20, lambda p: fold_centre(w1, rc1, cr1, p, mask1(p)))
            loop(1, 19, lambda p: fold_c(w1, f1, rc1, p, 1))
            arrived(w2_halo)
            loop(0, 12, lambda p: fold_centre(w2, rc2, cr2, p, mask2(p)))
            loop(1, 11, lambda p: fold_c(w2, f2, rc2, p, 2))
            gathered_all(w3, 0)
            fold_coarse()
        arrived(g1_halo[c])

        def source_1(p):
            big1[p] = rc1[p] * g1[c, p]

        loop(0, 20, source_1)

        def down_1(p):
            a1[p] = sweep_c(big1, big1, f1, p, 1)

        loop(1, 19, down_1)

        def restrict_1(i):
            total = None
            for dx in range(2):
                p = 2 + 2 * i + dx
                left = (sweep_c(a1, big1, f1, p, 1) - a1[p]) * cr1[p]
                total = left if total is None else total + left
            tmp[i] = total
            rows = tmp[i, pl.ds(4, 8, stride=2), :] + tmp[i, pl.ds(5, 8, stride=2), :]
            g2[2 + i, 2:10, :] = (rows + lane_swap(rows, 1)) * 0.125

        loop(0, 8, restrict_1)

        def source_2(p):
            big2[p] = rc2[p] * g2[p]

        loop(2, 10, source_2)

        def down_2(p):
            a2[p] = sweep_c(big2, big2, f2, p, 2)

        loop(3, 9, down_2)
        sums = []
        for xl in range(2):
            total = None
            for dx in range(2):
                p = 4 + 2 * xl + dx
                left = (sweep_c(a2, big2, f2, p, 2) - a2[p]) * cr2[p]
                total = left if total is None else total + left
            tmp[xl, 0:16, :] = (total + lane_swap(total, 2)) * 0.125
        cells = []
        for xl in range(2):
            for yl in range(2):
                cells.append(tmp[xl, pl.ds(4 + 2 * yl, 1), :] + tmp[xl, pl.ds(5 + 2 * yl, 1), :])
        g3row[c, 0] = pack_quads(cells)
        spread_all(g3row.at[c], g3.at[c], 1 + c)

        def keep_2(p):
            x2[c, 0, p, 4:8, :] = g2[p, 4:8, :]
            x2[c, 1, p, 4:8, :] = a2[p, 4:8, :]

        loop(4, 8, keep_2)
        start(x2_halo[c])

        gathered_all(g3.at[c], 1 + c)
        c3[1:17] = coarse_levels(g3[c, 0])

        quad8 = lax.rem(lane_index((8, 128)), 4)

        def widen_3(q):
            v = c3[b + lax.div(q, 2)]
            xl = lax.rem(q, 2)
            for yl in range(2):
                own = jnp.where(quad8 == 2 * xl + yl, v, 0.0)
                out = own
                pair = own + lane_swap(own, 1)
                out = pair + lane_swap(pair, 2)
                for dy in range(2):
                    t3[q, pl.ds(8 + 2 * yl + dy, 8, stride=4), :] = out

        loop(0, 6, widen_3)
        arrived(x2_halo[c])

        def correct_2(p):
            big2[p] = rc2[p] * x2[c, 0, p]
            add = t3[lax.div(p, 2), pl.ds(4 + 4 * g, 16), :]
            b2[p] = jnp.where(mask2(p), x2[c, 1, p] + add, 0.0)

        loop(0, 12, correct_2)

        def up_2a(p):
            a2[p] = sweep_c(b2, big2, f2, p, 2)

        loop(1, 11, up_2a)

        def up_2b(i):
            t2[i] = sweep_c(a2, big2, f2, i + 2, 2)
            rows = t2[i, 2:10, :]
            t1[i, pl.ds(4, 8, stride=2), :] = rows
            t1[i, pl.ds(5, 8, stride=2), :] = rows

        loop(0, 8, up_2b)

        def correct_1(p):
            b1[p] = jnp.where(mask1(p), a1[p] + t1[lax.div(p - 2, 2)], 0.0)

        loop(2, 18, correct_1)

        def up_1a(p):
            a1[p] = sweep_c(b1, big1, f1, p, 1)

        loop(3, 17, up_1a)

        def up_1b(i):
            tmp[i] = sweep_c(a1, big1, f1, i + 4, 1)
            rows = tmp[i, 6:18, :]
            s0[i, pl.ds(0, 12, stride=2), :] = rows
            s0[i, pl.ds(1, 12, stride=2), :] = rows

        loop(0, 12, up_1b)

        arrived(x0_halo[c])

        def correct_0(p):
            add = s0[lax.div(p, 2)]
            mask = mask0(p)
            for part in range(2):
                b0[part, p] = jnp.where(mask, x0[c, part, p] + add, 0.0)

        loop(1, 23, correct_0)

        def up_0a(p):
            a0[0, p], a0[1, p] = sweep_0(b0, p)

        loop(2, 22, up_0a)

        def up_0b(p):
            b0[0, p], b0[1, p] = sweep_0(a0, p)

        loop(3, 21, up_0b)

        if c + 1 < CYCLES:

            def update(p):
                parts = sweep_0(b0, p)
                for part in range(2):
                    left = (parts[part] - b0[part, p]) * cr0[part, p]
                    g0[c + 1, part, p, 4:20, :] = left[4:20]
                    sol_ref[p - 4, :, 128 * part : 128 * part + 128] = b0[part, p, 4:20, :]

            loop(4, 20, update)
            start(g0_halo[c + 1])

    def finish(p):
        parts = sweep_0(b0, p)
        lefts = [(parts[part] - b0[part, p]) * cr0[part, p] for part in range(2)]
        for part in range(2):
            res_ref[p - 4, :, 128 * part : 128 * part + 128] = lefts[part][4:20]
            sol_ref[p - 4, :, 128 * part : 128 * part + 128] += b0[part, p, 4:20, :]

    loop(4, 20, finish)
    zi = lax.broadcasted_iota(jnp.int32, (256, 256), 1)
    ci = lax.broadcasted_iota(jnp.int32, (256, 256), 0)
    parted = jnp.where(ci < 128, 2 * ci, 2 * ci - 255)
    joined = jnp.where(zi == parted, 1.0, 0.0).astype(jnp.bfloat16)
    for ref in (sol_ref, res_ref):
        ref[...] = split_dot(ref[...].reshape(256, 256), joined).reshape(16, 16, 256)

    for copy in pending:
        copy.wait_send()
    sent_all(dummy6, 0)
    for c in range(CYCLES):
        sent_all(dummy1, 1 + c)


def body(right_side, weights):
    vmem = pl.BlockSpec(memory_space=pltpu.VMEM)
    field = jax.ShapeDtypeStruct((16, 16, 256), F32)
    f0 = (24, 24, 128)
    f1 = (20, 24, 128)
    f2 = (12, 16, 128)
    f3 = (BLK, GRP, 128)

    def buf(*shape):
        return pltpu.VMEM(shape, F32)

    return pl.pallas_call(
        kernel,
        out_shape=(field, field),
        in_specs=[vmem, vmem],
        out_specs=(vmem, vmem),
        scratch_shapes=[
            buf(12, *f0), buf(12, *f0), buf(2, *f0), buf(2, *f0), buf(2, 2, *f0), buf(2, *f0),
            buf(2, *f0), buf(2, *f0), buf(2, 2, *f0), buf(12, 24, 128),
            buf(6, *f1), buf(6, *f1), buf(*f1), buf(*f1), buf(2, *f1), buf(*f1), buf(*f1), buf(*f1), buf(8, 24, 128),
            buf(6, *f2), buf(6, *f2), buf(*f2), buf(*f2), buf(*f2), buf(2, 2, *f2), buf(*f2), buf(*f2), buf(*f2),
            buf(8, 16, 128),
            buf(6, 1, 128), buf(6, *f3), buf(6, *f3), buf(*f3), buf(*f3), buf(2, 1, 1, 128), buf(2, 1, *f3),
            buf(18, 8, 128), buf(6, 48, 128),
            buf(6, *f3), buf(*f3), buf(12, 24, 128), buf(127, 6, 1, 128), buf(127, 1, 1, 128),
            pltpu.SemaphoreType.DMA((11, 8)),
            pltpu.SemaphoreType.DMA((11, 8)),
            pltpu.SemaphoreType.DMA((3,)),
            pltpu.SemaphoreType.DMA((3,)),
        ],
        compiler_params=pltpu.CompilerParams(
            collective_id=0, has_side_effects=True, vmem_limit_bytes=56 * 1024 * 1024
        ),
    )(right_side, weights)


def solution(mesh):
    return jax.shard_map(
        body,
        mesh=mesh,
        in_specs=(P("blk", "grp", None), P(None, "blk", "grp", None)),
        out_specs=(P("blk", "grp", None), P("blk", "grp", None)),
        check_vma=False,
    )
```

time: 980 us -> 106 us (0.11)
  the two profiles are of different devices: /device:TPU:104 before, /device:TPU:1 now
where the time goes in v1:
time: 106 us; the launch traced here: 105 us
  Pallas kernels  101 us (95%)
  local copies, waits for them, and re-layouts  3.34 us (3%)
    pallas_call x1, Pallas kernels, body(): pl.pallas_call(kernel, out_shape=(field, field), in_specs=[vmem, vmem], o...  101 us
    unnamed x2, local copies, waits for them, and re-layouts  3.34 us

profile of v1, /device:TPU:1, one launch (start us, length us, event | category | flops | bytes accessed | tf_op | source)
XLA Modules:
  0.0 105.5 jit_solution(14266172417518376926)
XLA Ops:
  0.6 101.5 %shard_map.41 = (f32[16,16,256]{2,1,0:T(8,128)}, f32[16,16,256]{2,1,0:T(8,128)}) custom-call(f32[16,16,256]{2,1,0:T(8,128)} %rhs_ref.1, f32[6,16,16,256]{3,2,1,0:T(8,128)} %w_ref.1), custom_call_target="tpu_custom_call" | custom-call | tf_op jit(solution)/shard_map/pallas_call | solution.py:611
  102.1 1.7 %copy.6 = f32[16,16,256]{2,1,0:T(8,128)} copy(f32[16,16,256]{2,1,0:T(8,128)} %get-tuple-element.4) | data formatting | bytes 524288
  103.8 1.7 %copy.7 = f32[16,16,256]{2,1,0:T(8,128)} copy(f32[16,16,256]{2,1,0:T(8,128)} %get-tuple-element.5) | data formatting | bytes 524288

commit v2 on v1

v2 whole, which is shorter than its diff:
```python
import functools

import jax
import jax.numpy as jnp
from jax import lax
from jax.experimental import pallas as pl
from jax.experimental.pallas import tpu as pltpu
from jax.sharding import PartitionSpec as P

MESH = pl.DeviceIdType.MESH
F32 = jnp.float32
BLK, GRP = 16, 8
OMEGA = 0.7
KEEP = 1.0 - OMEGA
NEIGHBOURS = tuple((dx, dy) for dx in (-1, 0, 1) for dy in (-1, 0, 1) if (dx, dy) != (0, 0))
CYCLES = 2


def lane_roll(v, n):
    return pltpu.roll(v, n % 128, v.ndim - 1)


def row_roll(v, n):
    axis = v.ndim - 2
    return pltpu.roll(v, n % v.shape[axis], axis)


def lane_index(shape):
    return lax.broadcasted_iota(jnp.int32, shape, len(shape) - 1)


def lane_swap(v, n):
    even = (lane_index(v.shape[-2:]) & n) == 0
    even = jnp.broadcast_to(even, v.shape)
    return jnp.where(even, lane_roll(v, -n), lane_roll(v, n))


def split_dot(x, matrix):
    high = x.astype(jnp.bfloat16)
    rest = x - high.astype(F32)
    middle = rest.astype(jnp.bfloat16)
    low = (rest - middle.astype(F32)).astype(jnp.bfloat16)
    dot = functools.partial(jnp.dot, preferred_element_type=F32)
    return (dot(low, matrix) + dot(middle, matrix)) + dot(high, matrix)


def span(delta, size, halo, start):
    if delta == 1:
        return pl.ds(start + size - halo, halo), pl.ds(start - halo, halo)
    if delta == -1:
        return pl.ds(start, halo), pl.ds(start + size, halo)
    return pl.ds(start, size), pl.ds(start, size)


def kernel(
    rhs_ref, w_ref, sol_ref, res_ref,
    w0, f0, rc0, cr0, g0, big0, a0, b0, x0, s0,
    w1, f1, rc1, cr1, g1, big1, a1, b1, t1,
    w2, f2, rc2, cr2, g2, x2, big2, a2, b2, t2,
    w3row, w3, f3, rc3, cr3, g3row, g3, c3, t3,
    f4, rc4, tmp, dummy6, dummy1,
    send_sem, recv_sem, all_send, all_recv,
):
    b = lax.axis_index("blk")
    g = lax.axis_index("grp")

    def device(dx, dy):
        return (lax.rem(b + dx + BLK, BLK), lax.rem(g + dy + GRP, GRP))

    barrier = pltpu.get_barrier_semaphore()

    def greet(k, carry):
        pl.semaphore_signal(
            barrier, inc=1, device_id=device(lax.div(k, GRP), lax.rem(k, GRP)), device_id_type=MESH
        )
        return carry

    lax.fori_loop(1, BLK * GRP, greet, 0)

    def loop(begin, end, step):
        def one(index, carry):
            step(index)
            return carry

        lax.fori_loop(begin, end, one, 0)

    def copies(view, lead, size, halo, start_x, start_y, slot):
        out = []
        for n, (dx, dy) in enumerate(NEIGHBOURS):
            sx, tx = span(dx, size, halo, start_x)
            sy, ty = span(dy, size, halo, start_y)
            out.append(
                pltpu.make_async_remote_copy(
                    src_ref=view.at[lead + (sx, sy)],
                    dst_ref=view.at[lead + (tx, ty)],
                    send_sem=send_sem.at[slot, n],
                    recv_sem=recv_sem.at[slot, n],
                    device_id=device(dx, dy),
                    device_id_type=MESH,
                )
            )
        return out

    pending = []

    def start(batch):
        for copy in batch:
            copy.start()
        pending.extend(batch)

    def arrived(batch):
        for copy in batch:
            copy.wait_recv()

    def spread_all(row, gathered, slot):
        mine = pltpu.make_async_copy(row, gathered.at[:, b, pl.ds(g, 1), :], all_recv.at[slot])
        mine.start()

        def send(k, carry):
            pltpu.make_async_remote_copy(
                src_ref=row,
                dst_ref=gathered.at[:, b, pl.ds(g, 1), :],
                send_sem=all_send.at[slot],
                recv_sem=all_recv.at[slot],
                device_id=device(lax.div(k, GRP), lax.rem(k, GRP)),
                device_id_type=MESH,
            ).start()
            return carry

        lax.fori_loop(1, BLK * GRP, send, 0)

    def gathered_all(gathered, slot):
        pltpu.make_async_copy(gathered, gathered, all_recv.at[slot]).wait()

    def sent_all(dummy, slot):
        pltpu.make_async_copy(dummy, dummy, all_send.at[slot]).wait()

    def inside(rows, size, start_x, start_y):
        def mask(p, n):
            shape = (n, rows, 128)
            x = lax.broadcasted_iota(jnp.int32, shape, 0) + (b * size + p - start_x)
            y = lax.broadcasted_iota(jnp.int32, shape, 1) + (g * size - start_y)
            ok_x = jnp.logical_and(x >= 0, x < BLK * size)
            ok_y = jnp.logical_and(y >= 0, y < GRP * size)
            return jnp.logical_and(ok_x, ok_y)

        return mask

    def planes(begin, end, size, step):
        count = (end - begin) // size
        if count == 1:
            step(begin, size)
        elif count > 1:
            loop(0, count, lambda i: step(begin + i * size, size))
        if end - begin > count * size:
            step(begin + count * size, end - begin - count * size)

    def pairs(v):
        both = v.reshape((v.shape[0] // 2, 2) + v.shape[1:])
        return both[:, 0] + both[:, 1]

    def doubled(v):
        wide = jnp.broadcast_to(v[:, None], (v.shape[0], 2) + v.shape[1:])
        return wide.reshape((2 * v.shape[0],) + v.shape[1:])

    zi = lax.broadcasted_iota(jnp.int32, (256, 256), 0)
    ci = lax.broadcasted_iota(jnp.int32, (256, 256), 1)
    parted = jnp.where(ci < 128, 2 * ci, 2 * ci - 255)
    split = jnp.where(zi == parted, 1.0, 0.0).astype(jnp.bfloat16)
    parts = split_dot(rhs_ref[...].reshape(256, 256), split)
    g0[0, 0, 4:20, 4:20, :] = parts[:, :128].reshape(16, 16, 128)
    g0[0, 1, 4:20, 4:20, :] = parts[:, 128:].reshape(16, 16, 128)

    def part_weights(k):
        both = split_dot(w_ref[k].reshape(256, 256), split)
        w0[2 * k, 4:20, 4:20, :] = both[:, :128].reshape(16, 16, 128)
        w0[2 * k + 1, 4:20, 4:20, :] = both[:, 128:].reshape(16, 16, 128)

    loop(0, 6, part_weights)

    pl.semaphore_wait(barrier, BLK * GRP - 1)

    all_of = slice(None)
    w0_halo = copies(w0, (all_of,), 16, 3, 4, 4, 0)
    g0_halo = [copies(g0, (c, all_of), 16, 2, 4, 4, 3 + c) for c in range(CYCLES)]
    x0_halo = [copies(x0, (c, all_of), 16, 3, 4, 4, 5 + c) for c in range(CYCLES)]
    w1_halo = copies(w1, (all_of,), 8, 6, 6, 8, 1)
    g1_halo = [copies(g1, (c,), 8, 6, 6, 8, 7 + c) for c in range(CYCLES)]
    w2_halo = copies(w2, (all_of,), 4, 4, 4, 4, 2)
    x2_halo = [copies(x2, (c, all_of), 4, 4, 4, 4, 9 + c) for c in range(CYCLES)]

    start(g0_halo[0])
    start(w0_halo)

    def weights_1(k):
        total = None
        for part in range(2):
            for dy in range(2):
                term = pairs(w0[2 * k + part, 4:20, pl.ds(4 + dy, 8, stride=2), :])
                total = term if total is None else total + term
        w1[k, 6:14, 8:16, :] = total * (1.0 / 32.0)

    loop(0, 6, weights_1)
    start(w1_halo)
    for k in range(6):
        total = None
        for dy in range(2):
            term = pairs(w1[k, 6:14, pl.ds(8 + dy, 4, stride=2), :])
            total = term if total is None else total + term
        w2[k, 4:8, 4:8, :] = (total + lane_swap(total, 1)) * (1.0 / 32.0)
    start(w2_halo)

    quad = lane_index((1, 128)) & 3

    def pack_quads(cells):
        out = cells[3]
        for n in range(3):
            out = jnp.where(quad == n, cells[n], out)
        return out

    for k in range(6):
        total = pairs(w2[k, 4:8, 4:8, :])
        total = (total + lane_swap(total, 2)) * (1.0 / 32.0)
        cells = []
        for xl in range(2):
            for yl in range(2):
                cells.append(total[xl, 2 * yl : 2 * yl + 1] + total[xl, 2 * yl + 1 : 2 * yl + 2])
        w3row[k] = pack_quads(cells)
    spread_all(w3row, w3, 0)

    mask0 = inside(24, 16, 4, 4)
    mask1 = inside(24, 8, 6, 8)
    mask2 = inside(16, 4, 4, 4)

    def relaxed(total, mask):
        return jnp.where(mask, OMEGA / total, 0.0)

    arrived(w0_halo)

    def fold_0(p, n):
        here, low, high = pl.ds(p, n), pl.ds(p - 1, n), pl.ds(p + 1, n)
        mask = mask0(p, n)
        lanes = lane_index((n, 24, 128))
        rc = []
        for part in range(2):
            total = w0[part, here]
            for k in range(1, 6):
                total = total + w0[2 * k + part, here]
            rc.append(relaxed(total, mask))
            rc0[part, here] = rc[part]
            cr0[part, here] = total * (1.0 / OMEGA)
            f0[0 + part, here] = rc[part] * w0[0 + part, low]
            f0[2 + part, here] = rc[part] * w0[2 + part, high]
            f0[4 + part, here] = rc[part] * row_roll(w0[4 + part, here], 1)
            f0[6 + part, here] = rc[part] * row_roll(w0[6 + part, here], -1)
        f0[8, here] = rc[0] * jnp.where(lanes == 0, 0.0, lane_roll(w0[9, here], 1))
        f0[9, here] = rc[1] * w0[8, here]
        f0[10, here] = rc[0] * w0[11, here]
        f0[11, here] = rc[1] * jnp.where(lanes == 127, 0.0, lane_roll(w0[10, here], -1))

    planes(2, 22, 5, fold_0)

    def sweep_0(u, p, n):
        here, low, high = pl.ds(p, n), pl.ds(p - 1, n), pl.ds(p + 1, n)
        e, o = u[0, here], u[1, here]
        out_e = KEEP * e + big0[0, here]
        out_o = KEEP * o + big0[1, here]
        out_e += f0[0, here] * u[0, low]
        out_o += f0[1, here] * u[1, low]
        out_e += f0[2, here] * u[0, high]
        out_o += f0[3, here] * u[1, high]
        out_e += f0[4, here] * row_roll(e, 1)
        out_o += f0[5, here] * row_roll(o, 1)
        out_e += f0[6, here] * row_roll(e, -1)
        out_o += f0[7, here] * row_roll(o, -1)
        out_e += f0[8, here] * lane_roll(o, 1)
        out_o += f0[9, here] * e
        out_e += f0[10, here] * o
        out_o += f0[11, here] * lane_roll(e, -1)
        return out_e, out_o

    def sweep_c(u, big, f, p, n, step):
        here = pl.ds(p, n)
        v = u[here]
        out = KEEP * v + big[here]
        out += f[0, here] * u[pl.ds(p - 1, n)]
        out += f[1, here] * u[pl.ds(p + 1, n)]
        out += f[2, here] * row_roll(v, 1)
        out += f[3, here] * row_roll(v, -1)
        out += f[4, here] * lane_roll(v, step)
        out += f[5, here] * lane_roll(v, -step)
        return out

    def fold_centre(w, rc, cr, p, n, mask):
        here = pl.ds(p, n)
        total = w[0, here]
        for k in range(1, 6):
            total = total + w[k, here]
        rc[here] = relaxed(total, mask)
        cr[here] = total * (1.0 / OMEGA)

    def fold_c(w, f, rc, p, n, step):
        here = pl.ds(p, n)
        r = rc[here]
        lanes = lane_index(r.shape)
        f[0, here] = r * w[0, pl.ds(p - 1, n)]
        f[1, here] = r * w[1, pl.ds(p + 1, n)]
        f[2, here] = r * row_roll(w[2, here], 1)
        f[3, here] = r * row_roll(w[3, here], -1)
        f[4, here] = r * jnp.where(lanes < step, 0.0, lane_roll(w[4, here], step))
        f[5, here] = r * jnp.where(lanes >= 128 - step, 0.0, lane_roll(w[5, here], -step))

    shape3 = (BLK, GRP, 128)

    def before(v):
        return jnp.concatenate([v[BLK - 1 :], v[: BLK - 1]], axis=0)

    def after(v):
        return jnp.concatenate([v[1:], v[:1]], axis=0)

    lane3 = lane_index(shape3)
    blk3 = lax.broadcasted_iota(jnp.int32, shape3, 0)
    grp3 = lax.broadcasted_iota(jnp.int32, shape3, 1)
    low_x = (lane3 & 2) == 0
    low_y = (lane3 & 1) == 0

    def shifts_3(v):
        r2, l2 = lane_roll(v, 2), lane_roll(v, -2)
        yield jnp.where(low_x, before(l2), r2)
        yield jnp.where(low_x, l2, after(r2))
        r1, l1 = lane_roll(v, 1), lane_roll(v, -1)
        yield jnp.where(low_y, row_roll(l1, 1), r1)
        yield jnp.where(low_y, l1, row_roll(r1, -1))
        yield lane_roll(v, 4)
        yield lane_roll(v, -4)

    def shifts_4(v):
        yield before(v)
        yield after(v)
        yield row_roll(v, 1)
        yield row_roll(v, -1)
        yield lane_roll(v, 8)
        yield lane_roll(v, -8)

    def octet(v):
        v = v + lane_swap(v, 1)
        v = v + lane_swap(v, 2)
        return v + lane_swap(v, 4)

    def fold_coarse():
        ws = [w3[k] for k in range(6)]
        total = ws[0] + ws[1] + ws[2] + ws[3] + ws[4] + ws[5]
        rc = OMEGA / total
        rc3[...] = rc
        cr3[...] = total * (1.0 / OMEGA)
        edge = (
            jnp.logical_and(blk3 == 0, low_x),
            jnp.logical_and(blk3 == BLK - 1, jnp.logical_not(low_x)),
            jnp.logical_and(grp3 == 0, low_y),
            jnp.logical_and(grp3 == GRP - 1, jnp.logical_not(low_y)),
            lane3 < 4,
            lane3 >= 124,
        )
        for k in range(6):
            moved = list(shifts_3(ws[k]))[k]
            f3[k] = jnp.where(edge[k], 0.0, rc * moved)
        total = None
        for k in range(6):
            coarse = octet(ws[k]) * (1.0 / 32.0)
            f4[k] = coarse
            total = coarse if total is None else total + coarse
        rc = OMEGA / total
        rc4[...] = rc
        edge = (blk3 == 0, blk3 == BLK - 1, grp3 == 0, grp3 == GRP - 1, lane3 < 8, lane3 >= 120)
        for k in range(6):
            moved = list(shifts_4(f4[k]))[k]
            f4[k] = jnp.where(edge[k], 0.0, rc * moved)

    def sweep_3(v, big):
        out = KEEP * v + big
        for k, moved in enumerate(shifts_3(v)):
            out += f3[k] * moved
        return out

    def sweep_4(v, big):
        out = KEEP * v + big
        for k, moved in enumerate(shifts_4(v)):
            out += f4[k] * moved
        return out

    def coarse_levels(source):
        big = rc3[...] * source
        u = sweep_3(big, big)
        left = (sweep_3(u, big) - u) * cr3[...]
        big_4 = rc4[...] * (octet(left) * 0.125)
        v = lax.fori_loop(0, 7, lambda n, v: sweep_4(v, big_4), big_4)
        u = u + v
        u = sweep_3(u, big)
        return sweep_3(u, big)

    for c in range(CYCLES):
        arrived(g0_halo[c])

        def source_0(p, n):
            here = pl.ds(p, n)
            for part in range(2):
                big0[part, here] = rc0[part, here] * g0[c, part, here]

        planes(2, 22, 10, source_0)

        def down_0(p, n):
            here = pl.ds(p, n)
            a0[0, here], a0[1, here] = sweep_0(big0, p, n)

        planes(3, 21, 9, down_0)

        def restrict_0(p, n):
            here = pl.ds(p, n)
            e, o = sweep_0(a0, p, n)
            left = (e - a0[0, here]) * cr0[0, here] + (o - a0[1, here]) * cr0[1, here]
            m = n // 2
            tmp[0:m] = pairs(left)
            rows = tmp[0:m, pl.ds(4, 8, stride=2), :] + tmp[0:m, pl.ds(5, 8, stride=2), :]
            g1[c, pl.ds(lax.div(p, 2) + 4, m), 8:16, :] = rows * 0.125

        planes(4, 20, 8, restrict_0)
        start(g1_halo[c])
        for part in range(2):
            x0[c, part, 4:20, 4:20, :] = a0[part, 4:20, 4:20, :]
        start(x0_halo[c])

        if c == 0:
            arrived(w1_halo)
            planes(0, 20, 10, lambda p, n: fold_centre(w1, rc1, cr1, p, n, mask1(p, n)))
            planes(1, 19, 6, lambda p, n: fold_c(w1, f1, rc1, p, n, 1))
            arrived(w2_halo)
            planes(0, 12, 12, lambda p, n: fold_centre(w2, rc2, cr2, p, n, mask2(p, n)))
            planes(1, 11, 10, lambda p, n: fold_c(w2, f2, rc2, p, n, 2))
            gathered_all(w3, 0)
            fold_coarse()
        arrived(g1_halo[c])
        big1[...] = rc1[...] * g1[c]
        a1[1:19] = sweep_c(big1, big1, f1, 1, 18, 1)
        left = (sweep_c(a1, big1, f1, 2, 16, 1) - a1[2:18]) * cr1[2:18]
        tmp[0:8] = pairs(left)
        rows = tmp[0:8, pl.ds(4, 8, stride=2), :] + tmp[0:8, pl.ds(5, 8, stride=2), :]
        g2[2:10, 2:10, :] = (rows + lane_swap(rows, 1)) * 0.125
        big2[2:10] = rc2[2:10] * g2[2:10]
        a2[3:9] = sweep_c(big2, big2, f2, 3, 6, 2)
        left = (sweep_c(a2, big2, f2, 4, 4, 2) - a2[4:8]) * cr2[4:8]
        left = pairs(left)
        tmp[0:2, 0:16, :] = (left + lane_swap(left, 2)) * 0.125
        cells = []
        for xl in range(2):
            for yl in range(2):
                cells.append(tmp[xl, pl.ds(4 + 2 * yl, 1), :] + tmp[xl, pl.ds(5 + 2 * yl, 1), :])
        g3row[c, 0] = pack_quads(cells)
        spread_all(g3row.at[c], g3.at[c], 1 + c)
        x2[c, 0, 4:8, 4:8, :] = g2[4:8, 4:8, :]
        x2[c, 1, 4:8, 4:8, :] = a2[4:8, 4:8, :]
        start(x2_halo[c])
        gathered_all(g3.at[c], 1 + c)
        c3[1:17] = coarse_levels(g3[c, 0])

        near = c3[pl.ds(b, 3)]
        quads = lane_index((3, 8, 128)) & 3
        for xl in range(2):
            for yl in range(2):
                own = jnp.where(quads == 2 * xl + yl, near, 0.0)
                own = own + lane_swap(own, 1)
                own = own + lane_swap(own, 2)
                for dy in range(2):
                    t3[:, xl, pl.ds(8 + 2 * yl + dy, 8, stride=4), :] = own
        arrived(x2_halo[c])
        big2[...] = rc2[...] * x2[c, 0]
        add = doubled(t3[:, :, pl.ds(4 + 4 * g, 16), :].reshape(6, 16, 128))
        b2[...] = jnp.where(mask2(0, 12), x2[c, 1] + add, 0.0)
        a2[1:11] = sweep_c(b2, big2, f2, 1, 10, 2)
        t2[...] = sweep_c(a2, big2, f2, 2, 8, 2)
        rows = t2[:, 2:10, :]
        t1[:, pl.ds(4, 8, stride=2), :] = rows
        t1[:, pl.ds(5, 8, stride=2), :] = rows

        b1[2:18] = jnp.where(mask1(2, 16), a1[2:18] + doubled(t1[...]), 0.0)
        a1[3:17] = sweep_c(b1, big1, f1, 3, 14, 1)
        tmp[...] = sweep_c(a1, big1, f1, 4, 12, 1)
        rows = tmp[:, 6:18, :]
        s0[:, pl.ds(0, 12, stride=2), :] = rows
        s0[:, pl.ds(1, 12, stride=2), :] = rows

        arrived(x0_halo[c])

        def correct_0(p, n):
            here = pl.ds(p, n)
            add = doubled(s0[pl.ds(lax.div(p, 2), n // 2)])
            mask = mask0(p, n)
            for part in range(2):
                b0[part, here] = jnp.where(mask, x0[c, part, here] + add, 0.0)

        planes(0, 24, 8, correct_0)

        def up_0a(p, n):
            here = pl.ds(p, n)
            a0[0, here], a0[1, here] = sweep_0(b0, p, n)

        planes(2, 22, 10, up_0a)

        def up_0b(p, n):
            here = pl.ds(p, n)
            b0[0, here], b0[1, here] = sweep_0(a0, p, n)

        planes(3, 21, 9, up_0b)

        def update(p, n):
            here, out = pl.ds(p, n), pl.ds(p - 4, n)
            swept = sweep_0(b0, p, n)
            for part in range(2):
                lanes = pl.ds(128 * part, 128)
                u = b0[part, here]
                left = ((swept[part] - u) * cr0[part, here])[:, 4:20, :]
                if c + 1 < CYCLES:
                    g0[c + 1, part, here, 4:20, :] = left
                else:
                    res_ref[out, :, lanes] = left
                u = u[:, 4:20, :]
                sol_ref[out, :, lanes] = u if c == 0 else sol_ref[out, :, lanes] + u

        planes(4, 20, 8, update)
        if c + 1 < CYCLES:
            start(g0_halo[c + 1])

    zi = lax.broadcasted_iota(jnp.int32, (256, 256), 1)
    ci = lax.broadcasted_iota(jnp.int32, (256, 256), 0)
    parted = jnp.where(ci < 128, 2 * ci, 2 * ci - 255)
    joined = jnp.where(zi == parted, 1.0, 0.0).astype(jnp.bfloat16)
    for ref in (sol_ref, res_ref):
        ref[...] = split_dot(ref[...].reshape(256, 256), joined).reshape(16, 16, 256)

    for copy in pending:
        copy.wait_send()
    sent_all(dummy6, 0)
    for c in range(CYCLES):
        sent_all(dummy1, 1 + c)


def body(right_side, weights):
    vmem = pl.BlockSpec(memory_space=pltpu.VMEM)
    field = jax.ShapeDtypeStruct((16, 16, 256), F32)
    f0 = (24, 24, 128)
    f1 = (20, 24, 128)
    f2 = (12, 16, 128)
    f3 = (BLK, GRP, 128)

    def buf(*shape):
        return pltpu.VMEM(shape, F32)

    return pl.pallas_call(
        kernel,
        out_shape=(field, field),
        in_specs=[vmem, vmem],
        out_specs=(vmem, vmem),
        scratch_shapes=[
            buf(12, *f0), buf(12, *f0), buf(2, *f0), buf(2, *f0), buf(2, 2, *f0), buf(2, *f0),
            buf(2, *f0), buf(2, *f0), buf(2, 2, *f0), buf(12, 24, 128),
            buf(6, *f1), buf(6, *f1), buf(*f1), buf(*f1), buf(2, *f1), buf(*f1), buf(*f1), buf(*f1), buf(8, 24, 128),
            buf(6, *f2), buf(6, *f2), buf(*f2), buf(*f2), buf(*f2), buf(2, 2, *f2), buf(*f2), buf(*f2), buf(*f2),
            buf(8, 16, 128),
            buf(6, 1, 128), buf(6, *f3), buf(6, *f3), buf(*f3), buf(*f3), buf(2, 1, 1, 128), buf(2, 1, *f3),
            buf(18, 8, 128), buf(3, 2, 48, 128),
            buf(6, *f3), buf(*f3), buf(12, 24, 128), buf(127, 6, 1, 128), buf(127, 1, 1, 128),
            pltpu.SemaphoreType.DMA((11, 8)),
            pltpu.SemaphoreType.DMA((11, 8)),
            pltpu.SemaphoreType.DMA((3,)),
            pltpu.SemaphoreType.DMA((3,)),
        ],
        compiler_params=pltpu.CompilerParams(
            collective_id=0, has_side_effects=True, vmem_limit_bytes=56 * 1024 * 1024
        ),
    )(right_side, weights)


def solution(mesh):
    return jax.shard_map(
        body,
        mesh=mesh,
        in_specs=(P("blk", "grp", None), P(None, "blk", "grp", None)),
        out_specs=(P("blk", "grp", None), P("blk", "grp", None)),
        check_vma=False,
    )
```

time: 106 us -> 84.2 us (0.79)
  Pallas kernels: 101 us -> 80 us
    pallas_call x1, Pallas kernels: 101 us -> 80 us  [body(): pl.pallas_call(kernel, out_shape=(field, field), in_specs=[vmem, vmem], o...]
where the time goes in v2:
time: 84.2 us; the launch traced here: 84 us
  Pallas kernels  80 us (95%)
  local copies, waits for them, and re-layouts  3.34 us (4%)
    pallas_call x1, Pallas kernels, body(): pl.pallas_call(kernel, out_shape=(field, field), in_specs=[vmem, vmem], o...  80 us
    unnamed x2, local copies, waits for them, and re-layouts  3.34 us

profile of v2, /device:TPU:1, one launch (start us, length us, event | category | flops | bytes accessed | tf_op | source)
XLA Modules:
  0.0 84.0 jit_solution(6260858264532020956)
XLA Ops:
  0.6 80.0 %shard_map.41 = (f32[16,16,256]{2,1,0:T(8,128)}, f32[16,16,256]{2,1,0:T(8,128)}) custom-call(f32[16,16,256]{2,1,0:T(8,128)} %rhs_ref.1, f32[6,16,16,256]{3,2,1,0:T(8,128)} %w_ref.1), custom_call_target="tpu_custom_call" | custom-call | tf_op jit(solution)/shard_map/pallas_call | solution.py:557
  80.6 1.7 %copy.6 = f32[16,16,256]{2,1,0:T(8,128)} copy(f32[16,16,256]{2,1,0:T(8,128)} %get-tuple-element.4) | data formatting | bytes 524288
  82.3 1.7 %copy.7 = f32[16,16,256]{2,1,0:T(8,128)} copy(f32[16,16,256]{2,1,0:T(8,128)} %get-tuple-element.5) | data formatting | bytes 524288

commit v3 on v2

--- a/solution.py
+++ b/solution.py
@@ -12,7 +12,17 @@
 BLK, GRP = 16, 8
 OMEGA = 0.7
 KEEP = 1.0 - OMEGA
-NEIGHBOURS = tuple((dx, dy) for dx in (-1, 0, 1) for dy in (-1, 0, 1) if (dx, dy) != (0, 0))
+FACES = ((1, 0), (-1, 0), (0, 1), (0, -1))
+CORNERS = ((1, 1), (1, -1), (-1, 1), (-1, -1))
+
+
+def distance(offset):
+    dx, dy = offset
+    x, y, z = dx % 4, dy // 2, dx // 4
+    return min(x, 4 - x) + min(y, 4 - y) + min(z, 4 - z)
+
+
+EVERYONE = sorted(((dx, dy) for dx in range(BLK) for dy in range(GRP) if dx or dy), key=distance, reverse=True)
 CYCLES = 2
 
 
@@ -44,25 +54,30 @@
     return (dot(low, matrix) + dot(middle, matrix)) + dot(high, matrix)
 
 
-def span(delta, size, halo, start):
+def piece(delta, size, start, first, count):
     if delta == 1:
-        return pl.ds(start + size - halo, halo), pl.ds(start - halo, halo)
+        return pl.ds(start + size + 1 - first - count, count), pl.ds(start + 1 - first - count, count)
     if delta == -1:
-        return pl.ds(start, halo), pl.ds(start + size, halo)
+        return pl.ds(start + first - 1, count), pl.ds(start + size + first - 1, count)
     return pl.ds(start, size), pl.ds(start, size)
 
 
 def kernel(
     rhs_ref, w_ref, sol_ref, res_ref,
-    w0, f0, rc0, cr0, g0, big0, a0, b0, x0, s0,
+    raw, w0, f0, cr0, g0, big0, a0, b0, x0, s0,
     w1, f1, rc1, cr1, g1, big1, a1, b1, t1,
     w2, f2, rc2, cr2, g2, x2, big2, a2, b2, t2,
-    w3row, w3, f3, rc3, cr3, g3row, g3, c3, t3,
-    f4, rc4, tmp, dummy6, dummy1,
-    send_sem, recv_sem, all_send, all_recv,
+    w3, f3, rc3, cr3, g3row, g3, c3, t3,
+    f4, rc4, tmp, dummy, dummy1,
+    load_sem, send_sem, recv_sem, all_send, all_recv,
 ):
     b = lax.axis_index("blk")
     g = lax.axis_index("grp")
+
+    loads = [pltpu.make_async_copy(w_ref.at[k], raw.at[k], load_sem.at[k]) for k in range(6)]
+    loads.append(pltpu.make_async_copy(rhs_ref, raw.at[6], load_sem.at[6]))
+    for copy in loads:
+        copy.start()
 
     def device(dx, dy):
         return (lax.rem(b + dx + BLK, BLK), lax.rem(g + dy + GRP, GRP))
@@ -84,56 +99,74 @@
 
         lax.fori_loop(begin, end, one, 0)
 
-    def copies(view, lead, size, halo, start_x, start_y, slot):
-        out = []
-        for n, (dx, dy) in enumerate(NEIGHBOURS):
-            sx, tx = span(dx, size, halo, start_x)
-            sy, ty = span(dy, size, halo, start_y)
-            out.append(
-                pltpu.make_async_remote_copy(
-                    src_ref=view.at[lead + (sx, sy)],
-                    dst_ref=view.at[lead + (tx, ty)],
-                    send_sem=send_sem.at[slot, n],
-                    recv_sem=recv_sem.at[slot, n],
-                    device_id=device(dx, dy),
-                    device_id_type=MESH,
-                )
+    def patch(view, lead, fields, level, dx, dy, layers_x, layers_y):
+        size, start_x, start_y = level
+        sx, tx = piece(dx, size, start_x, *layers_x)
+        sy, ty = piece(dy, size, start_y, *layers_y)
+        rows = fields * (layers_x[1] if dx else size) * (layers_y[1] if dy else size)
+        return view.at[lead + (sx, sy)], view.at[lead + (tx, ty)], device(dx, dy), rows
+
+    def faces(view, lead, fields, level, layers):
+        return [
+            patch(view, lead, fields, level, dx, dy, (1, layers), (1, layers)) for dx, dy in FACES
+        ]
+
+    def corners(view, lead, fields, level, layers_x, layers_y):
+        return [patch(view, lead, fields, level, dx, dy, layers_x, layers_y) for dx, dy in CORNERS]
+
+    def inward(view, each, level, layer):
+        return [
+            patch(view, (pl.ds(k * each, each),), each, level, dx, dy, (layer, 1), (layer, 1))
+            for k, (dx, dy) in enumerate(FACES)
+        ]
+
+    batches = []
+
+    def batch(parts):
+        index = len(batches)
+        copies = [
+            pltpu.make_async_remote_copy(
+                src_ref=src,
+                dst_ref=dst,
+                send_sem=send_sem.at[index],
+                recv_sem=recv_sem.at[index],
+                device_id=to,
+                device_id_type=MESH,
             )
-        return out
-
-    pending = []
-
-    def start(batch):
-        for copy in batch:
+            for src, dst, to, _ in parts
+        ]
+        rows = sum(part[3] for part in parts)
+        batches.append((copies, dummy.at[pl.ds(0, rows)], index))
+        return batches[-1]
+
+    def start(one):
+        for copy in one[0]:
             copy.start()
-        pending.extend(batch)
-
-    def arrived(batch):
-        for copy in batch:
-            copy.wait_recv()
-
-    def spread_all(row, gathered, slot):
-        mine = pltpu.make_async_copy(row, gathered.at[:, b, pl.ds(g, 1), :], all_recv.at[slot])
-        mine.start()
-
-        def send(k, carry):
+
+    def arrived(one):
+        pltpu.make_async_copy(one[1], one[1], recv_sem.at[one[2]]).wait()
+
+    def departed(one):
+        pltpu.make_async_copy(one[1], one[1], send_sem.at[one[2]]).wait()
+
+    def spread(src, dst, offsets, slot):
+        for dx, dy in offsets:
             pltpu.make_async_remote_copy(
-                src_ref=row,
-                dst_ref=gathered.at[:, b, pl.ds(g, 1), :],
+                src_ref=src,
+                dst_ref=dst,
                 send_sem=all_send.at[slot],
                 recv_sem=all_recv.at[slot],
-                device_id=device(lax.div(k, GRP), lax.rem(k, GRP)),
+                device_id=device(dx, dy),
                 device_id_type=MESH,
             ).start()
-            return carry
-
-        lax.fori_loop(1, BLK * GRP, send, 0)
-
-    def gathered_all(gathered, slot):
-        pltpu.make_async_copy(gathered, gathered, all_recv.at[slot]).wait()
-
-    def sent_all(dummy, slot):
-        pltpu.make_async_copy(dummy, dummy, all_send.at[slot]).wait()
+
+    def spread_all(c):
+        row, mine = g3row.at[c], g3.at[c, b, pl.ds(g, 1), :]
+        pltpu.make_async_copy(row, mine, all_recv.at[2 + c]).start()
+        spread(row, mine, EVERYONE, 2 + c)
+
+    def wait_for(ref, sem):
+        pltpu.make_async_copy(ref, ref, sem).wait()
 
     def inside(rows, size, start_x, start_y):
         def mask(p, n):
@@ -167,27 +200,46 @@
     ci = lax.broadcasted_iota(jnp.int32, (256, 256), 1)
     parted = jnp.where(ci < 128, 2 * ci, 2 * ci - 255)
     split = jnp.where(zi == parted, 1.0, 0.0).astype(jnp.bfloat16)
-    parts = split_dot(rhs_ref[...].reshape(256, 256), split)
-    g0[0, 0, 4:20, 4:20, :] = parts[:, :128].reshape(16, 16, 128)
-    g0[0, 1, 4:20, 4:20, :] = parts[:, 128:].reshape(16, 16, 128)
 
     def part_weights(k):
-        both = split_dot(w_ref[k].reshape(256, 256), split)
+        pltpu.make_async_copy(w_ref.at[k], raw.at[k], load_sem.at[k]).wait()
+        both = split_dot(raw[k].reshape(256, 256), split)
         w0[2 * k, 4:20, 4:20, :] = both[:, :128].reshape(16, 16, 128)
         w0[2 * k + 1, 4:20, 4:20, :] = both[:, 128:].reshape(16, 16, 128)
 
     loop(0, 6, part_weights)
+    loads[6].wait()
+    both = split_dot(raw[6].reshape(256, 256), split)
+    for part in range(2):
+        total = w0[part, 4:20, 4:20, :]
+        for k in range(1, 6):
+            total = total + w0[2 * k + part, 4:20, 4:20, :]
+        source = both[:, 128 * part : 128 * part + 128].reshape(16, 16, 128)
+        g0[0, part, 4:20, 4:20, :] = (OMEGA / total) * source
 
     pl.semaphore_wait(barrier, BLK * GRP - 1)
 
-    all_of = slice(None)
-    w0_halo = copies(w0, (all_of,), 16, 3, 4, 4, 0)
-    g0_halo = [copies(g0, (c, all_of), 16, 2, 4, 4, 3 + c) for c in range(CYCLES)]
-    x0_halo = [copies(x0, (c, all_of), 16, 3, 4, 4, 5 + c) for c in range(CYCLES)]
-    w1_halo = copies(w1, (all_of,), 8, 6, 6, 8, 1)
-    g1_halo = [copies(g1, (c,), 8, 6, 6, 8, 7 + c) for c in range(CYCLES)]
-    w2_halo = copies(w2, (all_of,), 4, 4, 4, 4, 2)
-    x2_halo = [copies(x2, (c, all_of), 4, 4, 4, 4, 9 + c) for c in range(CYCLES)]
+    every = slice(None)
+    level_0, level_1, level_2 = (16, 4, 4), (8, 6, 8), (4, 4, 4)
+
+    def halo(view, lead, fields, level, layers, corner):
+        return faces(view, lead, fields, level, layers) + corners(
+            view, lead, fields, level, (1, corner), (1, corner)
+        )
+
+    cycles = range(CYCLES)
+    g0_halo = [batch(halo(g0, (c, every), 2, level_0, 2, 1)) for c in cycles]
+    g1_halo = [batch(halo(g1, (c,), 1, level_1, 6, 5)) for c in cycles]
+    x0_halo = [batch(halo(x0, (c, every), 2, level_0, 3, 2)) for c in cycles]
+    x2_halo = [batch(halo(x2, (c, every), 2, level_2, 4, 4)) for c in cycles]
+    w0_halo = batch(halo(w0, (every,), 12, level_0, 2, 2) + inward(w0, 2, level_0, 3))
+    w1_halo = batch(
+        halo(w1, (every,), 6, level_1, 5, 3)
+        + inward(w1, 1, level_1, 6)
+        + corners(w1, (every,), 6, level_1, (4, 2), (1, 2))
+        + corners(w1, (every,), 6, level_1, (1, 2), (4, 2))
+    )
+    w2_halo = batch(halo(w2, (every,), 6, level_2, 3, 4) + inward(w2, 1, level_2, 4))
 
     start(g0_halo[0])
     start(w0_halo)
@@ -202,13 +254,16 @@
 
     loop(0, 6, weights_1)
     start(w1_halo)
+    total = w1[0, 6:14, 8:16, :]
+    for k in range(1, 6):
+        total = total + w1[k, 6:14, 8:16, :]
+    rc1[...] = OMEGA / total
     for k in range(6):
         total = None
         for dy in range(2):
             term = pairs(w1[k, 6:14, pl.ds(8 + dy, 4, stride=2), :])
             total = term if total is None else total + term
         w2[k, 4:8, 4:8, :] = (total + lane_swap(total, 1)) * (1.0 / 32.0)
-    start(w2_halo)
 
     quad = lane_index((1, 128)) & 3
 
@@ -225,8 +280,9 @@
         for xl in range(2):
             for yl in range(2):
                 cells.append(total[xl, 2 * yl : 2 * yl + 1] + total[xl, 2 * yl + 1 : 2 * yl + 2])
-        w3row[k] = pack_quads(cells)
-    spread_all(w3row, w3, 0)
+        w3[k, b, pl.ds(g, 1), :] = pack_quads(cells)
+    mine = w3.at[:, b, pl.ds(g, 1), :]
+    spread(mine, mine, [(0, dy) for dy in range(1, GRP)], 0)
 
     mask0 = inside(24, 16, 4, 4)
     mask1 = inside(24, 8, 6, 8)
@@ -247,7 +303,6 @@
             for k in range(1, 6):
                 total = total + w0[2 * k + part, here]
             rc.append(relaxed(total, mask))
-            rc0[part, here] = rc[part]
             cr0[part, here] = total * (1.0 / OMEGA)
             f0[0 + part, here] = rc[part] * w0[0 + part, low]
             f0[2 + part, here] = rc[part] * w0[2 + part, high]
@@ -291,17 +346,13 @@
         out += f[5, here] * lane_roll(v, -step)
         return out
 
-    def fold_centre(w, rc, cr, p, n, mask):
+    def fold_c(w, f, cr, p, n, step, mask):
         here = pl.ds(p, n)
         total = w[0, here]
         for k in range(1, 6):
             total = total + w[k, here]
-        rc[here] = relaxed(total, mask)
+        r = relaxed(total, mask)
         cr[here] = total * (1.0 / OMEGA)
-
-    def fold_c(w, f, rc, p, n, step):
-        here = pl.ds(p, n)
-        r = rc[here]
         lanes = lane_index(r.shape)
         f[0, here] = r * w[0, pl.ds(p - 1, n)]
         f[1, here] = r * w[1, pl.ds(p + 1, n)]
@@ -309,6 +360,7 @@
         f[3, here] = r * row_roll(w[3, here], -1)
         f[4, here] = r * jnp.where(lanes < step, 0.0, lane_roll(w[4, here], step))
         f[5, here] = r * jnp.where(lanes >= 128 - step, 0.0, lane_roll(w[5, here], -step))
+        return r
 
     shape3 = (BLK, GRP, 128)
 
@@ -403,8 +455,9 @@
 
         def source_0(p, n):
             here = pl.ds(p, n)
+            mask = mask0(p, n)
             for part in range(2):
-                big0[part, here] = rc0[part, here] * g0[c, part, here]
+                big0[part, here] = jnp.where(mask, g0[c, part, here], 0.0)
 
         planes(2, 22, 10, source_0)
 
@@ -421,7 +474,9 @@
             m = n // 2
             tmp[0:m] = pairs(left)
             rows = tmp[0:m, pl.ds(4, 8, stride=2), :] + tmp[0:m, pl.ds(5, 8, stride=2), :]
-            g1[c, pl.ds(lax.div(p, 2) + 4, m), 8:16, :] = rows * 0.125
+            here = pl.ds(lax.div(p, 2) - 2, m)
+            there = pl.ds(lax.div(p, 2) + 4, m)
+            g1[c, there, 8:16, :] = rc1[here] * (rows * 0.125)
 
         planes(4, 20, 8, restrict_0)
         start(g1_halo[c])
@@ -430,21 +485,22 @@
         start(x0_halo[c])
 
         if c == 0:
+            start(w2_halo)
+            wait_for(w3.at[:, pl.ds(0, GRP - 1), pl.ds(0, 1), :], all_recv.at[0])
+            block = w3.at[:, b]
+            spread(block, block, [(dx, 0) for dx in range(1, BLK)], 1)
             arrived(w1_halo)
-            planes(0, 20, 10, lambda p, n: fold_centre(w1, rc1, cr1, p, n, mask1(p, n)))
-            planes(1, 19, 6, lambda p, n: fold_c(w1, f1, rc1, p, n, 1))
-            arrived(w2_halo)
-            planes(0, 12, 12, lambda p, n: fold_centre(w2, rc2, cr2, p, n, mask2(p, n)))
-            planes(1, 11, 10, lambda p, n: fold_c(w2, f2, rc2, p, n, 2))
-            gathered_all(w3, 0)
-            fold_coarse()
+            planes(1, 19, 6, lambda p, n: fold_c(w1, f1, cr1, p, n, 1, mask1(p, n)))
         arrived(g1_halo[c])
-        big1[...] = rc1[...] * g1[c]
+        big1[...] = jnp.where(mask1(0, 20), g1[c], 0.0)
         a1[1:19] = sweep_c(big1, big1, f1, 1, 18, 1)
         left = (sweep_c(a1, big1, f1, 2, 16, 1) - a1[2:18]) * cr1[2:18]
         tmp[0:8] = pairs(left)
         rows = tmp[0:8, pl.ds(4, 8, stride=2), :] + tmp[0:8, pl.ds(5, 8, stride=2), :]
         g2[2:10, 2:10, :] = (rows + lane_swap(rows, 1)) * 0.125
+        if c == 0:
+            arrived(w2_halo)
+            rc2[1:11] = fold_c(w2, f2, cr2, 1, 10, 2, mask2(1, 10))
         big2[2:10] = rc2[2:10] * g2[2:10]
         a2[3:9] = sweep_c(big2, big2, f2, 3, 6, 2)
         left = (sweep_c(a2, big2, f2, 4, 4, 2) - a2[4:8]) * cr2[4:8]
@@ -454,13 +510,16 @@
         for xl in range(2):
             for yl in range(2):
                 cells.append(tmp[xl, pl.ds(4 + 2 * yl, 1), :] + tmp[xl, pl.ds(5 + 2 * yl, 1), :])
-        g3row[c, 0] = pack_quads(cells)
-        spread_all(g3row.at[c], g3.at[c], 1 + c)
-        x2[c, 0, 4:8, 4:8, :] = g2[4:8, 4:8, :]
+        g3row[c] = pack_quads(cells)
+        spread_all(c)
+        x2[c, 0, 4:8, 4:8, :] = big2[4:8, 4:8, :]
         x2[c, 1, 4:8, 4:8, :] = a2[4:8, 4:8, :]
         start(x2_halo[c])
-        gathered_all(g3.at[c], 1 + c)
-        c3[1:17] = coarse_levels(g3[c, 0])
+        if c == 0:
+            wait_for(w3.at[:, pl.ds(0, BLK - 1)], all_recv.at[1])
+            fold_coarse()
+        wait_for(g3.at[c], all_recv.at[2 + c])
+        c3[1:17] = coarse_levels(g3[c])
 
         near = c3[pl.ds(b, 3)]
         quads = lane_index((3, 8, 128)) & 3
@@ -472,9 +531,10 @@
                 for dy in range(2):
                     t3[:, xl, pl.ds(8 + 2 * yl + dy, 8, stride=4), :] = own
         arrived(x2_halo[c])
-        big2[...] = rc2[...] * x2[c, 0]
+        inside_2 = mask2(0, 12)
+        big2[...] = jnp.where(inside_2, x2[c, 0], 0.0)
         add = doubled(t3[:, :, pl.ds(4 + 4 * g, 16), :].reshape(6, 16, 128))
-        b2[...] = jnp.where(mask2(0, 12), x2[c, 1] + add, 0.0)
+        b2[...] = jnp.where(inside_2, x2[c, 1] + add, 0.0)
         a2[1:11] = sweep_c(b2, big2, f2, 1, 10, 2)
         t2[...] = sweep_c(a2, big2, f2, 2, 8, 2)
         rows = t2[:, 2:10, :]
@@ -517,11 +577,11 @@
             for part in range(2):
                 lanes = pl.ds(128 * part, 128)
                 u = b0[part, here]
-                left = ((swept[part] - u) * cr0[part, here])[:, 4:20, :]
+                change = swept[part] - u
                 if c + 1 < CYCLES:
-                    g0[c + 1, part, here, 4:20, :] = left
+                    g0[c + 1, part, here, 4:20, :] = change[:, 4:20, :]
                 else:
-                    res_ref[out, :, lanes] = left
+                    res_ref[out, :, lanes] = (change * cr0[part, here])[:, 4:20, :]
                 u = u[:, 4:20, :]
                 sol_ref[out, :, lanes] = u if c == 0 else sol_ref[out, :, lanes] + u
 
@@ -536,11 +596,12 @@
     for ref in (sol_ref, res_ref):
         ref[...] = split_dot(ref[...].reshape(256, 256), joined).reshape(16, 16, 256)
 
-    for copy in pending:
-        copy.wait_send()
-    sent_all(dummy6, 0)
-    for c in range(CYCLES):
-        sent_all(dummy1, 1 + c)
+    for one in batches:
+        departed(one)
+    wait_for(w3.at[:, pl.ds(0, GRP - 1), pl.ds(0, 1), :], all_send.at[0])
+    wait_for(w3.at[:, pl.ds(0, BLK - 1)], all_send.at[1])
+    for c in cycles:
+        wait_for(dummy1, all_send.at[2 + c])
 
 
 def body(right_side, weights):
@@ -557,21 +618,23 @@
     return pl.pallas_call(
         kernel,
         out_shape=(field, field),
-        in_specs=[vmem, vmem],
+        in_specs=[pl.BlockSpec(memory_space=pl.ANY)] * 2,
         out_specs=(vmem, vmem),
         scratch_shapes=[
-            buf(12, *f0), buf(12, *f0), buf(2, *f0), buf(2, *f0), buf(2, 2, *f0), buf(2, *f0),
+            buf(7, 16, 16, 256),
+            buf(12, *f0), buf(12, *f0), buf(2, *f0), buf(2, 2, *f0), buf(2, *f0),
             buf(2, *f0), buf(2, *f0), buf(2, 2, *f0), buf(12, 24, 128),
-            buf(6, *f1), buf(6, *f1), buf(*f1), buf(*f1), buf(2, *f1), buf(*f1), buf(*f1), buf(*f1), buf(8, 24, 128),
+            buf(6, *f1), buf(6, *f1), buf(8, 8, 128), buf(*f1), buf(2, *f1), buf(*f1), buf(*f1), buf(*f1), buf(8, 24, 128),
             buf(6, *f2), buf(6, *f2), buf(*f2), buf(*f2), buf(*f2), buf(2, 2, *f2), buf(*f2), buf(*f2), buf(*f2),
             buf(8, 16, 128),
-            buf(6, 1, 128), buf(6, *f3), buf(6, *f3), buf(*f3), buf(*f3), buf(2, 1, 1, 128), buf(2, 1, *f3),
+            buf(6, *f3), buf(6, *f3), buf(*f3), buf(*f3), buf(2, 1, 128), buf(2, *f3),
             buf(18, 8, 128), buf(3, 2, 48, 128),
-            buf(6, *f3), buf(*f3), buf(12, 24, 128), buf(127, 6, 1, 128), buf(127, 1, 1, 128),
-            pltpu.SemaphoreType.DMA((11, 8)),
-            pltpu.SemaphoreType.DMA((11, 8)),
-            pltpu.SemaphoreType.DMA((3,)),
-            pltpu.SemaphoreType.DMA((3,)),
+            buf(6, *f3), buf(*f3), buf(12, 24, 128), buf(2048, 128), buf(127, 1, 128),
+            pltpu.SemaphoreType.DMA((7,)),
+            pltpu.SemaphoreType.DMA((11,)),
+            pltpu.SemaphoreType.DMA((11,)),
+            pltpu.SemaphoreType.DMA((4,)),
+            pltpu.SemaphoreType.DMA((4,)),
         ],
         compiler_params=pltpu.CompilerParams(
             collective_id=0, has_side_effects=True, vmem_limit_bytes=56 * 1024 * 1024

time: 84.2 us -> 69.6 us (0.83)
  Pallas kernels: 80 us -> 65.4 us
    pallas_call x1, Pallas kernels: 80 us -> 65.4 us  [body(): pl.pallas_call(kernel, out_shape=(field, field), in_specs=[pl.BlockSpec(m...]
where the time goes in v3:
time: 69.6 us; the launch traced here: 69.4 us
  Pallas kernels  65.4 us (94%)
  local copies, waits for them, and re-layouts  3.34 us (5%)
    pallas_call x1, Pallas kernels, body(): pl.pallas_call(kernel, out_shape=(field, field), in_specs=[pl.BlockSpec(m...  65.4 us
    unnamed x2, local copies, waits for them, and re-layouts  3.34 us

profile of v3, /device:TPU:1, one launch (start us, length us, event | category | flops | bytes accessed | tf_op | source)
XLA Modules:
  0.0 69.4 jit_solution(8085823265919282181)
XLA Ops:
  0.6 65.4 %shard_map.41 = (f32[16,16,256]{2,1,0:T(8,128)}, f32[16,16,256]{2,1,0:T(8,128)}) custom-call(f32[16,16,256]{2,1,0:T(8,128)} %rhs_ref.1, f32[6,16,16,256]{3,2,1,0:T(8,128)} %w_ref.1), custom_call_target="tpu_custom_call" | custom-call | tf_op jit(solution)/shard_map/pallas_call | solution.py:618
  66.0 1.7 %copy.6 = f32[16,16,256]{2,1,0:T(8,128)} copy(f32[16,16,256]{2,1,0:T(8,128)} %get-tuple-element.4) | data formatting | bytes 524288
  67.7 1.7 %copy.7 = f32[16,16,256]{2,1,0:T(8,128)} copy(f32[16,16,256]{2,1,0:T(8,128)} %get-tuple-element.5) | data formatting | bytes 524288

commit v4 on v3

--- a/solution.py
+++ b/solution.py
@@ -68,7 +68,7 @@
     w1, f1, rc1, cr1, g1, big1, a1, b1, t1,
     w2, f2, rc2, cr2, g2, x2, big2, a2, b2, t2,
     w3, f3, rc3, cr3, g3row, g3, c3, t3,
-    f4, rc4, tmp, dummy, dummy1,
+    f4, rc4, tmp, dummy, dummy1, w0x,
     load_sem, send_sem, recv_sem, all_send, all_recv,
 ):
     b = lax.axis_index("blk")
@@ -84,13 +84,17 @@
 
     barrier = pltpu.get_barrier_semaphore()
 
-    def greet(k, carry):
-        pl.semaphore_signal(
-            barrier, inc=1, device_id=device(lax.div(k, GRP), lax.rem(k, GRP)), device_id_type=MESH
-        )
+    def greet(dx, dy):
+        pl.semaphore_signal(barrier, inc=1, device_id=device(dx, dy), device_id_type=MESH)
+
+    def greet_block(dx, carry):
+        for dy in range(GRP):
+            greet(dx, dy)
         return carry
 
-    lax.fori_loop(1, BLK * GRP, greet, 0)
+    for dy in range(1, GRP):
+        greet(0, dy)
+    lax.fori_loop(1, BLK, greet_block, 0)
 
     def loop(begin, end, step):
         def one(index, carry):
@@ -99,24 +103,25 @@
 
         lax.fori_loop(begin, end, one, 0)
 
-    def patch(view, lead, fields, level, dx, dy, layers_x, layers_y):
+    def patch(view, lead, fields, level, dx, dy, layers_x, layers_y, into=None):
+        into = view if into is None else into
         size, start_x, start_y = level
         sx, tx = piece(dx, size, start_x, *layers_x)
         sy, ty = piece(dy, size, start_y, *layers_y)
         rows = fields * (layers_x[1] if dx else size) * (layers_y[1] if dy else size)
-        return view.at[lead + (sx, sy)], view.at[lead + (tx, ty)], device(dx, dy), rows
-
-    def faces(view, lead, fields, level, layers):
+        return view.at[lead + (sx, sy)], into.at[lead + (tx, ty)], device(dx, dy), rows
+
+    def faces(view, lead, fields, level, layers, into=None):
+        return [patch(view, lead, fields, level, dx, dy, layers, layers, into) for dx, dy in FACES]
+
+    def corners(view, lead, fields, level, layers_x, layers_y, into=None):
         return [
-            patch(view, lead, fields, level, dx, dy, (1, layers), (1, layers)) for dx, dy in FACES
+            patch(view, lead, fields, level, dx, dy, layers_x, layers_y, into) for dx, dy in CORNERS
         ]
 
-    def corners(view, lead, fields, level, layers_x, layers_y):
-        return [patch(view, lead, fields, level, dx, dy, layers_x, layers_y) for dx, dy in CORNERS]
-
-    def inward(view, each, level, layer):
+    def inward(view, each, level, layer, into=None):
         return [
-            patch(view, (pl.ds(k * each, each),), each, level, dx, dy, (layer, 1), (layer, 1))
+            patch(view, (pl.ds(k * each, each),), each, level, dx, dy, (layer, 1), (layer, 1), into)
             for k, (dx, dy) in enumerate(FACES)
         ]
 
@@ -201,13 +206,16 @@
     parted = jnp.where(ci < 128, 2 * ci, 2 * ci - 255)
     split = jnp.where(zi == parted, 1.0, 0.0).astype(jnp.bfloat16)
 
-    def part_weights(k):
-        pltpu.make_async_copy(w_ref.at[k], raw.at[k], load_sem.at[k]).wait()
-        both = split_dot(raw[k].reshape(256, 256), split)
-        w0[2 * k, 4:20, 4:20, :] = both[:, :128].reshape(16, 16, 128)
-        w0[2 * k + 1, 4:20, 4:20, :] = both[:, 128:].reshape(16, 16, 128)
-
-    loop(0, 6, part_weights)
+    def part_weights(i):
+        first = 3 * i
+        for k in range(3):
+            pltpu.make_async_copy(w_ref.at[first + k], raw.at[first + k], load_sem.at[first + k]).wait()
+        both = split_dot(raw[pl.ds(first, 3)].reshape(768, 256), split).reshape(3, 16, 16, 256)
+        for k in range(3):
+            for part in range(2):
+                w0[2 * (first + k) + part, 4:20, 4:20, :] = both[k, :, :, 128 * part : 128 * part + 128]
+
+    loop(0, 2, part_weights)
     loads[6].wait()
     both = split_dot(raw[6].reshape(256, 256), split)
     for part in range(2):
@@ -223,7 +231,7 @@
     level_0, level_1, level_2 = (16, 4, 4), (8, 6, 8), (4, 4, 4)
 
     def halo(view, lead, fields, level, layers, corner):
-        return faces(view, lead, fields, level, layers) + corners(
+        return faces(view, lead, fields, level, (1, layers)) + corners(
             view, lead, fields, level, (1, corner), (1, corner)
         )
 
@@ -232,7 +240,12 @@
     g1_halo = [batch(halo(g1, (c,), 1, level_1, 6, 5)) for c in cycles]
     x0_halo = [batch(halo(x0, (c, every), 2, level_0, 3, 2)) for c in cycles]
     x2_halo = [batch(halo(x2, (c, every), 2, level_2, 4, 4)) for c in cycles]
-    w0_halo = batch(halo(w0, (every,), 12, level_0, 2, 2) + inward(w0, 2, level_0, 3))
+    w0_halo = batch(halo(w0, (every,), 12, level_0, 1, 1) + inward(w0, 2, level_0, 2))
+    w0_rest = batch(
+        faces(w0, (every,), 12, level_0, (2, 1), w0x)
+        + corners(w0, (every,), 12, level_0, (1, 2), (1, 2), w0x)
+        + inward(w0, 2, level_0, 3, w0x)
+    )
     w1_halo = batch(
         halo(w1, (every,), 6, level_1, 5, 3)
         + inward(w1, 1, level_1, 6)
@@ -313,7 +326,20 @@
         f0[10, here] = rc[0] * w0[11, here]
         f0[11, here] = rc[1] * jnp.where(lanes == 127, 0.0, lane_roll(w0[10, here], -1))
 
-    planes(2, 22, 5, fold_0)
+    planes(3, 21, 6, fold_0)
+
+    def merge_0():
+        for x in (2, 21):
+            w0[:, x, 4:20, :] = w0x[:, x, 4:20, :]
+        for y in (2, 21):
+            w0[:, 4:20, y : y + 1, :] = w0x[:, 4:20, y : y + 1, :]
+        for x in (2, 20):
+            for y in (2, 20):
+                w0[:, x : x + 2, y : y + 2, :] = w0x[:, x : x + 2, y : y + 2, :]
+        w0[0:2, 1, 4:20, :] = w0x[0:2, 1, 4:20, :]
+        w0[2:4, 22, 4:20, :] = w0x[2:4, 22, 4:20, :]
+        w0[4:6, 4:20, 1:2, :] = w0x[4:6, 4:20, 1:2, :]
+        w0[6:8, 4:20, 22:23, :] = w0x[6:8, 4:20, 22:23, :]
 
     def sweep_0(u, p, n):
         here, low, high = pl.ds(p, n), pl.ds(p - 1, n), pl.ds(p + 1, n)
@@ -377,12 +403,18 @@
     low_y = (lane3 & 1) == 0
 
     def shifts_3(v):
-        r2, l2 = lane_roll(v, 2), lane_roll(v, -2)
-        yield jnp.where(low_x, before(l2), r2)
-        yield jnp.where(low_x, l2, after(r2))
-        r1, l1 = lane_roll(v, 1), lane_roll(v, -1)
-        yield jnp.where(low_y, row_roll(l1, 1), r1)
-        yield jnp.where(low_y, l1, row_roll(r1, -1))
+        moved = lane_roll(v, 2)
+        yield moved
+        yield after(moved)
+        moved = lane_roll(v, -2)
+        yield moved
+        yield before(moved)
+        moved = lane_roll(v, 1)
+        yield moved
+        yield row_roll(moved, -1)
+        moved = lane_roll(v, -1)
+        yield moved
+        yield row_roll(moved, 1)
         yield lane_roll(v, 4)
         yield lane_roll(v, -4)
 
@@ -405,17 +437,22 @@
         rc = OMEGA / total
         rc3[...] = rc
         cr3[...] = total * (1.0 / OMEGA)
-        edge = (
-            jnp.logical_and(blk3 == 0, low_x),
-            jnp.logical_and(blk3 == BLK - 1, jnp.logical_not(low_x)),
-            jnp.logical_and(grp3 == 0, low_y),
-            jnp.logical_and(grp3 == GRP - 1, jnp.logical_not(low_y)),
-            lane3 < 4,
-            lane3 >= 124,
+        high_x, high_y = jnp.logical_not(low_x), jnp.logical_not(low_y)
+        uses = (
+            (0, high_x),
+            (1, jnp.logical_and(high_x, blk3 < BLK - 1)),
+            (1, low_x),
+            (0, jnp.logical_and(low_x, blk3 > 0)),
+            (2, high_y),
+            (3, jnp.logical_and(high_y, grp3 < GRP - 1)),
+            (3, low_y),
+            (2, jnp.logical_and(low_y, grp3 > 0)),
+            (4, lane3 >= 4),
+            (5, lane3 < 124),
         )
-        for k in range(6):
-            moved = list(shifts_3(ws[k]))[k]
-            f3[k] = jnp.where(edge[k], 0.0, rc * moved)
+        for n, (k, used) in enumerate(uses):
+            moved = list(shifts_3(ws[k]))[n]
+            f3[n] = jnp.where(used, rc * moved, 0.0)
         total = None
         for k in range(6):
             coarse = octet(ws[k]) * (1.0 / 32.0)
@@ -445,7 +482,7 @@
         u = sweep_3(big, big)
         left = (sweep_3(u, big) - u) * cr3[...]
         big_4 = rc4[...] * (octet(left) * 0.125)
-        v = lax.fori_loop(0, 7, lambda n, v: sweep_4(v, big_4), big_4)
+        v = lax.fori_loop(0, 7, lambda n, v: sweep_4(v, big_4), big_4, unroll=True)
         u = u + v
         u = sweep_3(u, big)
         return sweep_3(u, big)
@@ -489,6 +526,7 @@
             wait_for(w3.at[:, pl.ds(0, GRP - 1), pl.ds(0, 1), :], all_recv.at[0])
             block = w3.at[:, b]
             spread(block, block, [(dx, 0) for dx in range(1, BLK)], 1)
+            start(w0_rest)
             arrived(w1_halo)
             planes(1, 19, 6, lambda p, n: fold_c(w1, f1, cr1, p, n, 1, mask1(p, n)))
         arrived(g1_halo[c])
@@ -518,6 +556,9 @@
         if c == 0:
             wait_for(w3.at[:, pl.ds(0, BLK - 1)], all_recv.at[1])
             fold_coarse()
+            arrived(w0_rest)
+            merge_0()
+            planes(2, 22, 5, fold_0)
         wait_for(g3.at[c], all_recv.at[2 + c])
         c3[1:17] = coarse_levels(g3[c])
 
@@ -589,19 +630,29 @@
         if c + 1 < CYCLES:
             start(g0_halo[c + 1])
 
-    zi = lax.broadcasted_iota(jnp.int32, (256, 256), 1)
-    ci = lax.broadcasted_iota(jnp.int32, (256, 256), 0)
-    parted = jnp.where(ci < 128, 2 * ci, 2 * ci - 255)
-    joined = jnp.where(zi == parted, 1.0, 0.0).astype(jnp.bfloat16)
-    for ref in (sol_ref, res_ref):
-        ref[...] = split_dot(ref[...].reshape(256, 256), joined).reshape(16, 16, 256)
-
     for one in batches:
         departed(one)
     wait_for(w3.at[:, pl.ds(0, GRP - 1), pl.ds(0, 1), :], all_send.at[0])
     wait_for(w3.at[:, pl.ds(0, BLK - 1)], all_send.at[1])
     for c in cycles:
         wait_for(dummy1, all_send.at[2 + c])
+
+
+def join_kernel(sol_in, res_in, sol_out, res_out, halves, whole, load_sem, store_sem):
+    loads = [pltpu.make_async_copy(ref, halves.at[n], load_sem.at[n]) for n, ref in enumerate((sol_in, res_in))]
+    stores = [pltpu.make_async_copy(whole.at[n], ref, store_sem.at[n]) for n, ref in enumerate((sol_out, res_out))]
+    for copy in loads:
+        copy.start()
+    zi = lax.broadcasted_iota(jnp.int32, (256, 256), 1)
+    ci = lax.broadcasted_iota(jnp.int32, (256, 256), 0)
+    parted = jnp.where(ci < 128, 2 * ci, 2 * ci - 255)
+    joined = jnp.where(zi == parted, 1.0, 0.0).astype(jnp.bfloat16)
+    for n in range(2):
+        loads[n].wait()
+        whole[n] = split_dot(halves[n].reshape(256, 256), joined).reshape(16, 16, 256)
+        stores[n].start()
+    for copy in stores:
+        copy.wait()
 
 
 def body(right_side, weights):
@@ -615,7 +666,7 @@
     def buf(*shape):
         return pltpu.VMEM(shape, F32)
 
-    return pl.pallas_call(
+    parted = pl.pallas_call(
         kernel,
         out_shape=(field, field),
         in_specs=[pl.BlockSpec(memory_space=pl.ANY)] * 2,
@@ -627,12 +678,12 @@
             buf(6, *f1), buf(6, *f1), buf(8, 8, 128), buf(*f1), buf(2, *f1), buf(*f1), buf(*f1), buf(*f1), buf(8, 24, 128),
             buf(6, *f2), buf(6, *f2), buf(*f2), buf(*f2), buf(*f2), buf(2, 2, *f2), buf(*f2), buf(*f2), buf(*f2),
             buf(8, 16, 128),
-            buf(6, *f3), buf(6, *f3), buf(*f3), buf(*f3), buf(2, 1, 128), buf(2, *f3),
+            buf(6, *f3), buf(10, *f3), buf(*f3), buf(*f3), buf(2, 1, 128), buf(2, *f3),
             buf(18, 8, 128), buf(3, 2, 48, 128),
-            buf(6, *f3), buf(*f3), buf(12, 24, 128), buf(2048, 128), buf(127, 1, 128),
+            buf(6, *f3), buf(*f3), buf(12, 24, 128), buf(2048, 128), buf(127, 1, 128), buf(12, *f0),
             pltpu.SemaphoreType.DMA((7,)),
-            pltpu.SemaphoreType.DMA((11,)),
-            pltpu.SemaphoreType.DMA((11,)),
+            pltpu.SemaphoreType.DMA((12,)),
+            pltpu.SemaphoreType.DMA((12,)),
             pltpu.SemaphoreType.DMA((4,)),
             pltpu.SemaphoreType.DMA((4,)),
         ],
@@ -640,6 +691,16 @@
             collective_id=0, has_side_effects=True, vmem_limit_bytes=56 * 1024 * 1024
         ),
     )(right_side, weights)
+    return pl.pallas_call(
+        join_kernel,
+        out_shape=(field, field),
+        in_specs=[pl.BlockSpec(memory_space=pltpu.HBM)] * 2,
+        out_specs=[pl.BlockSpec(memory_space=pltpu.HBM)] * 2,
+        scratch_shapes=[
+            buf(2, 16, 16, 256), buf(2, 16, 16, 256), pltpu.SemaphoreType.DMA((2,)), pltpu.SemaphoreType.DMA((2,)),
+        ],
+        compiler_params=pltpu.CompilerParams(vmem_limit_bytes=60 * 1024 * 1024),
+    )(*parted)
 
 
 def solution(mesh):

time: 69.6 us -> 66.1 us (0.950)
  local copies, waits for them, and re-layouts: 3.34 us -> 0 us
    unnamed x2 -> x0, local copies, waits for them, and re-layouts: 3.34 us -> none
    pallas_call x1, Pallas kernels: 65.4 us -> 62.9 us  [body(): pl.pallas_call(kernel, out_shape=(field, field), in_specs=[pl.BlockSpec(m...]
    pallas_call x0 -> x1, Pallas kernels: none -> 2.38 us  [body(): pl.pallas_call(join_kernel, out_shape=(field, field), in_specs=[pl.BlockS...]
where the time goes in v4:
time: 66.1 us; the launch traced here: 65.9 us
  Pallas kernels  65.3 us (99%)
    pallas_call x1, Pallas kernels, body(): pl.pallas_call(kernel, out_shape=(field, field), in_specs=[pl.BlockSpec(m...  62.9 us
    pallas_call x1, Pallas kernels, body(): pl.pallas_call(join_kernel, out_shape=(field, field), in_specs=[pl.BlockS...  2.38 us

profile of v4, /device:TPU:1, one launch (start us, length us, event | category | flops | bytes accessed | tf_op | source)
XLA Modules:
  0.0 65.9 jit_solution(3111905797773422663)
XLA Ops:
  0.6 62.9 %shard_map.41 = (f32[16,16,256]{2,1,0:T(8,128)}, f32[16,16,256]{2,1,0:T(8,128)}) custom-call(f32[16,16,256]{2,1,0:T(8,128)} %rhs_ref.1, f32[6,16,16,256]{3,2,1,0:T(8,128)} %w_ref.1), custom_call_target="tpu_custom_call" | custom-call | tf_op jit(solution)/shard_map/pallas_call | solution.py:669
  63.6 2.4 %shard_map.42 = (f32[16,16,256]{2,1,0:T(8,128)}, f32[16,16,256]{2,1,0:T(8,128)}) custom-call(f32[16,16,256]{2,1,0:T(8,128)} %get-tuple-element.4.sol_in, f32[16,16,256]{2,1,0:T(8,128)} %get-tuple-element.5.res_in), custom_call_target="tpu_custom_call" | custom-call | tf_op jit(solution)/shard_map/pallas_call | solution.py:694

commit v5 on v4

--- a/solution.py
+++ b/solution.py
@@ -216,14 +216,6 @@
                 w0[2 * (first + k) + part, 4:20, 4:20, :] = both[k, :, :, 128 * part : 128 * part + 128]
 
     loop(0, 2, part_weights)
-    loads[6].wait()
-    both = split_dot(raw[6].reshape(256, 256), split)
-    for part in range(2):
-        total = w0[part, 4:20, 4:20, :]
-        for k in range(1, 6):
-            total = total + w0[2 * k + part, 4:20, 4:20, :]
-        source = both[:, 128 * part : 128 * part + 128].reshape(16, 16, 128)
-        g0[0, part, 4:20, 4:20, :] = (OMEGA / total) * source
 
     pl.semaphore_wait(barrier, BLK * GRP - 1)
 
@@ -231,8 +223,8 @@
     level_0, level_1, level_2 = (16, 4, 4), (8, 6, 8), (4, 4, 4)
 
     def halo(view, lead, fields, level, layers, corner):
-        return faces(view, lead, fields, level, (1, layers)) + corners(
-            view, lead, fields, level, (1, corner), (1, corner)
+        return corners(view, lead, fields, level, (1, corner), (1, corner)) + faces(
+            view, lead, fields, level, (1, layers)
         )
 
     cycles = range(CYCLES)
@@ -254,8 +246,16 @@
     )
     w2_halo = batch(halo(w2, (every,), 6, level_2, 3, 4) + inward(w2, 1, level_2, 4))
 
+    start(w0_halo)
+    loads[6].wait()
+    both = split_dot(raw[6].reshape(256, 256), split)
+    for part in range(2):
+        total = w0[part, 4:20, 4:20, :]
+        for k in range(1, 6):
+            total = total + w0[2 * k + part, 4:20, 4:20, :]
+        source = both[:, 128 * part : 128 * part + 128].reshape(16, 16, 128)
+        g0[0, part, 4:20, 4:20, :] = (OMEGA / total) * source
     start(g0_halo[0])
-    start(w0_halo)
 
     def weights_1(k):
         total = None
@@ -326,7 +326,7 @@
         f0[10, here] = rc[0] * w0[11, here]
         f0[11, here] = rc[1] * jnp.where(lanes == 127, 0.0, lane_roll(w0[10, here], -1))
 
-    planes(3, 21, 6, fold_0)
+    planes(3, 21, 9, fold_0)
 
     def merge_0():
         for x in (2, 21):
@@ -496,13 +496,13 @@
             for part in range(2):
                 big0[part, here] = jnp.where(mask, g0[c, part, here], 0.0)
 
-        planes(2, 22, 10, source_0)
+        planes(2, 22, 20, source_0)
 
         def down_0(p, n):
             here = pl.ds(p, n)
             a0[0, here], a0[1, here] = sweep_0(big0, p, n)
 
-        planes(3, 21, 9, down_0)
+        planes(3, 21, 18, down_0)
 
         def restrict_0(p, n):
             here = pl.ds(p, n)
@@ -511,11 +511,11 @@
             m = n // 2
             tmp[0:m] = pairs(left)
             rows = tmp[0:m, pl.ds(4, 8, stride=2), :] + tmp[0:m, pl.ds(5, 8, stride=2), :]
-            here = pl.ds(lax.div(p, 2) - 2, m)
-            there = pl.ds(lax.div(p, 2) + 4, m)
+            here = pl.ds((p // 2) - 2, m)
+            there = pl.ds((p // 2) + 4, m)
             g1[c, there, 8:16, :] = rc1[here] * (rows * 0.125)
 
-        planes(4, 20, 8, restrict_0)
+        planes(4, 20, 16, restrict_0)
         start(g1_halo[c])
         for part in range(2):
             x0[c, part, 4:20, 4:20, :] = a0[part, 4:20, 4:20, :]
@@ -593,24 +593,24 @@
 
         def correct_0(p, n):
             here = pl.ds(p, n)
-            add = doubled(s0[pl.ds(lax.div(p, 2), n // 2)])
+            add = doubled(s0[pl.ds((p // 2), n // 2)])
             mask = mask0(p, n)
             for part in range(2):
                 b0[part, here] = jnp.where(mask, x0[c, part, here] + add, 0.0)
 
-        planes(0, 24, 8, correct_0)
+        planes(0, 24, 24, correct_0)
 
         def up_0a(p, n):
             here = pl.ds(p, n)
             a0[0, here], a0[1, here] = sweep_0(b0, p, n)
 
-        planes(2, 22, 10, up_0a)
+        planes(2, 22, 20, up_0a)
 
         def up_0b(p, n):
             here = pl.ds(p, n)
             b0[0, here], b0[1, here] = sweep_0(a0, p, n)
 
-        planes(3, 21, 9, up_0b)
+        planes(3, 21, 18, up_0b)
 
         def update(p, n):
             here, out = pl.ds(p, n), pl.ds(p - 4, n)
@@ -626,7 +626,7 @@
                 u = u[:, 4:20, :]
                 sol_ref[out, :, lanes] = u if c == 0 else sol_ref[out, :, lanes] + u
 
-        planes(4, 20, 8, update)
+        planes(4, 20, 16, update)
         if c + 1 < CYCLES:
             start(g0_halo[c + 1])
 
@@ -638,18 +638,14 @@
         wait_for(dummy1, all_send.at[2 + c])
 
 
-def join_kernel(sol_in, res_in, sol_out, res_out, halves, whole, load_sem, store_sem):
-    loads = [pltpu.make_async_copy(ref, halves.at[n], load_sem.at[n]) for n, ref in enumerate((sol_in, res_in))]
+def join_kernel(sol_in, res_in, sol_out, res_out, whole, store_sem):
     stores = [pltpu.make_async_copy(whole.at[n], ref, store_sem.at[n]) for n, ref in enumerate((sol_out, res_out))]
-    for copy in loads:
-        copy.start()
     zi = lax.broadcasted_iota(jnp.int32, (256, 256), 1)
     ci = lax.broadcasted_iota(jnp.int32, (256, 256), 0)
     parted = jnp.where(ci < 128, 2 * ci, 2 * ci - 255)
     joined = jnp.where(zi == parted, 1.0, 0.0).astype(jnp.bfloat16)
-    for n in range(2):
-        loads[n].wait()
-        whole[n] = split_dot(halves[n].reshape(256, 256), joined).reshape(16, 16, 256)
+    for n, ref in enumerate((sol_in, res_in)):
+        whole[n] = split_dot(ref[...].reshape(256, 256), joined).reshape(16, 16, 256)
         stores[n].start()
     for copy in stores:
         copy.wait()
@@ -668,7 +664,7 @@
 
     parted = pl.pallas_call(
         kernel,
-        out_shape=(field, field),
+        out_shape=(buf(16, 16, 256), buf(16, 16, 256)),
         in_specs=[pl.BlockSpec(memory_space=pl.ANY)] * 2,
         out_specs=(vmem, vmem),
         scratch_shapes=[
@@ -694,12 +690,12 @@
     return pl.pallas_call(
         join_kernel,
         out_shape=(field, field),
-        in_specs=[pl.BlockSpec(memory_space=pltpu.HBM)] * 2,
+        in_specs=[vmem, vmem],
         out_specs=[pl.BlockSpec(memory_space=pltpu.HBM)] * 2,
         scratch_shapes=[
-            buf(2, 16, 16, 256), buf(2, 16, 16, 256), pltpu.SemaphoreType.DMA((2,)), pltpu.SemaphoreType.DMA((2,)),
+            buf(2, 16, 16, 256), pltpu.SemaphoreType.DMA((2,)),
         ],
-        compiler_params=pltpu.CompilerParams(vmem_limit_bytes=60 * 1024 * 1024),
+        compiler_params=pltpu.CompilerParams(vmem_limit_bytes=48 * 1024 * 1024),
     )(*parted)
 
 

time: 66.1 us -> 63.6 us (0.962)
  Pallas kernels: 65.3 us -> 62.8 us
    pallas_call x2, Pallas kernels: 65.3 us -> 62.8 us  [the longest x1 61.6 us: body(): pl.pallas_call(kernel, out_shape=(buf(16, 16, 256), buf(16, 16, 256)), in...]
where the time goes in v5:
time: 63.6 us; the launch traced here: 63.5 us
  Pallas kernels  62.8 us (99%)
  between operations  0.64 us (1%)
    pallas_call x1, Pallas kernels, body(): pl.pallas_call(kernel, out_shape=(buf(16, 16, 256), buf(16, 16, 256)), in...  61.6 us

profile of v5, /device:TPU:1, one launch (start us, length us, event | category | flops | bytes accessed | tf_op | source)
XLA Modules:
  0.0 63.5 jit_solution(14131523850291493369)
XLA Ops:
  0.6 61.6 %shard_map.41 = (f32[16,16,256]{2,1,0:T(8,128)S(1)}, f32[16,16,256]{2,1,0:T(8,128)S(1)}) custom-call(f32[16,16,256]{2,1,0:T(8,128)} %rhs_ref.1, f32[6,16,16,256]{3,2,1,0:T(8,128)} %w_ref.1), custom_call_target="tpu_custom_call" | custom-call | tf_op jit(solution)/shard_map/pallas_call | solution.py:665
  62.3 1.2 %shard_map.42 = (f32[16,16,256]{2,1,0:T(8,128)}, f32[16,16,256]{2,1,0:T(8,128)}) custom-call(f32[16,16,256]{2,1,0:T(8,128)S(1)} %get-tuple-element.4.sol_in, f32[16,16,256]{2,1,0:T(8,128)S(1)} %get-tuple-element.5.res_in), custom_call_target="tpu_custom_call" | custom-call | tf_op jit(solution)/shard_map/pallas_call | solution.py:690

commit v6 on v5

--- a/solution.py
+++ b/solution.py
@@ -526,10 +526,11 @@
             wait_for(w3.at[:, pl.ds(0, GRP - 1), pl.ds(0, 1), :], all_recv.at[0])
             block = w3.at[:, b]
             spread(block, block, [(dx, 0) for dx in range(1, BLK)], 1)
-            start(w0_rest)
             arrived(w1_halo)
             planes(1, 19, 6, lambda p, n: fold_c(w1, f1, cr1, p, n, 1, mask1(p, n)))
         arrived(g1_halo[c])
+        if c == 0:
+            start(w0_rest)
         big1[...] = jnp.where(mask1(0, 20), g1[c], 0.0)
         a1[1:19] = sweep_c(big1, big1, f1, 1, 18, 1)
         left = (sweep_c(a1, big1, f1, 2, 16, 1) - a1[2:18]) * cr1[2:18]

time: 63.6 us -> 63.6 us (level)
  no operation moved by 1% of the time
where the time goes in v6:
time: 63.6 us; the launch traced here: 63.5 us
  Pallas kernels  62.8 us (99%)
  between operations  0.64 us (1%)
    pallas_call x1, Pallas kernels, body(): pl.pallas_call(kernel, out_shape=(buf(16, 16, 256), buf(16, 16, 256)), in...  61.6 us

profile of v6, /device:TPU:1, one launch (start us, length us, event | category | flops | bytes accessed | tf_op | source)
XLA Modules:
  0.0 63.5 jit_solution(12380974174237395157)
XLA Ops:
  0.6 61.6 %shard_map.41 = (f32[16,16,256]{2,1,0:T(8,128)S(1)}, f32[16,16,256]{2,1,0:T(8,128)S(1)}) custom-call(f32[16,16,256]{2,1,0:T(8,128)} %rhs_ref.1, f32[6,16,16,256]{3,2,1,0:T(8,128)} %w_ref.1), custom_call_target="tpu_custom_call" | custom-call | tf_op jit(solution)/shard_map/pallas_call | solution.py:666
  62.3 1.2 %shard_map.42 = (f32[16,16,256]{2,1,0:T(8,128)}, f32[16,16,256]{2,1,0:T(8,128)}) custom-call(f32[16,16,256]{2,1,0:T(8,128)S(1)} %get-tuple-element.4.sol_in, f32[16,16,256]{2,1,0:T(8,128)S(1)} %get-tuple-element.5.res_in), custom_call_target="tpu_custom_call" | custom-call | tf_op jit(solution)/shard_map/pallas_call | solution.py:691
